TPU v7x, 32 devices: a whole 2x2x4 slice. The times are simulated.
32 devices in a mesh: fsdp: 32 (over z, y, x, core).
Axes of the slice: x: 2, y: 2, z: 4, core: 2. Of those that a mesh axis runs over, the one named last changes fastest.
Arguments:
- images: bfloat16 [256, 196, 768], P('fsdp'), may hold values from -6 to 6
- cotangent: bfloat16 [256, 196, 768], P('fsdp'), may hold values from -6 to 6
- counts: int32 [32], P('fsdp'), may hold values from 1 to 8, as said below
- w_token_in: float32 [75264], P('fsdp'), may hold values from -0.4375 to 0.4375
- w_token_out: float32 [75264], P('fsdp'), may hold values from -0.3125 to 0.3125
- w_chan_in: float32 [2359296], P('fsdp'), may hold values from -0.21875 to 0.21875
- w_chan_out: float32 [2359296], P('fsdp'), may hold values from -0.109375 to 0.109375
- gains: float32 [2, 768], replicated, may hold values from 0.4 to 1.8
- row_states: float32 [4420], replicated
- col_states: float32 [4420], replicated
- gain_states: float32 [2, 768], replicated, may hold values from 7056 to 28224
Outputs:
- block_out: float32 [256, 196, 768], P('fsdp')
- grad_input: float32 [256, 196, 768], P('fsdp')
- grad_token_in: float32 [75264], P('fsdp')
- grad_token_out: float32 [75264], P('fsdp')
- grad_chan_in: float32 [2359296], P('fsdp')
- grad_chan_out: float32 [2359296], P('fsdp')
- new_token_in: float32 [75264], P('fsdp')
- new_token_out: float32 [75264], P('fsdp')
- new_chan_in: float32 [2359296], P('fsdp')
- new_chan_out: float32 [2359296], P('fsdp')
- gain_grads: float32 [2, 768], replicated
- gain_stats: float32 [2, 768], replicated
- new_gains: float32 [2, 768], replicated
- row_stats: float32 [4420], replicated
- col_stats: float32 [4420], replicated
- update_rms: float32 [6], replicated
Inputs may be any that keep to these rules, and one draw needn't show every extreme that they name: `counts`: slots of a device at or past its count are padding; the first device holds one image and the last is full.
All inputs are finite; a program needn't handle non-finite values.
Results may differ from a plain program's by a relative error of at most 0.0081.
Values may be sent and summed in bfloat16 or wider, within the bound.
No kernel may reach another device: no remote copies, remote signals or barrier semaphores. Data moves between devices by JAX's collectives and lax.ppermute only.
A program may use at most 256 MiB of HBM per device.

v0:
```python
import jax
import jax.numpy as jnp
from jax import lax
from jax.sharding import PartitionSpec as P

D = 768
PATCH_COUNT = 196
TOKEN_HIDDEN = 384
DC = 3072
MICRO = 2


decay_rate = 0.5
clip_level = 0.5
step_rate = 1.0


def normalize(values):
    centred = values - jnp.mean(values, axis=-1, keepdims=True)
    spread = jnp.mean(centred * centred, axis=-1, keepdims=True)
    inverse = lax.rsqrt(spread + 1e-06)
    return (centred * inverse, inverse)


def norm_back(grad_norm, normed, inverse):
    first = jnp.mean(grad_norm, axis=-1, keepdims=True)
    second = jnp.mean(grad_norm * normed, axis=-1, keepdims=True)
    return inverse * (grad_norm - first - normed * second)


def factor_sums(values, offset_at, row_count, col_count):
    length = values.shape[0]
    covered = length // col_count + 2
    buffer = jnp.zeros((covered * col_count,), jnp.float32)
    buffer = lax.dynamic_update_slice(buffer, values, (offset_at % col_count,))
    buffer_grid = buffer.reshape(covered, col_count)
    row_part = jnp.sum(buffer_grid, axis=1)
    col_part = jnp.sum(buffer_grid, axis=0)
    row_full = lax.dynamic_update_slice(
        jnp.zeros((row_count + covered,), jnp.float32), row_part, (offset_at // col_count,)
    )
    return (row_full[:row_count], col_part)


def expand(row_vec, col_vec, offset_at, length):
    col_count = col_vec.shape[0]
    covered = length // col_count + 2
    padded = jnp.concatenate([row_vec, jnp.ones((covered,), jnp.float32)])
    rows_here = lax.dynamic_slice(padded, (offset_at // col_count,), (covered,))
    whole = (rows_here[:, None] * col_vec[None, :]).reshape(-1)
    return lax.dynamic_slice(whole, (offset_at % col_count,), (length,))


def gelu_back(pre, grad):
    return jax.vjp(jax.nn.gelu, pre)[1](grad)[0]


def shards(
    images,
    cotangent,
    counts,
    w_token_in,
    w_token_out,
    w_chan_in,
    w_chan_out,
    gains,
    row_states,
    col_states,
    gain_states,
):
    count_dev = images.shape[0]
    micro_rows = count_dev // MICRO
    slot_ids = jnp.arange(count_dev, dtype=jnp.int32)
    keep_all = (slot_ids < counts[0]).astype(jnp.float32)[:, None, None]
    low_copies = (
        w_token_in.astype(jnp.bfloat16),
        w_token_out.astype(jnp.bfloat16),
        w_chan_in.astype(jnp.bfloat16),
        w_chan_out.astype(jnp.bfloat16),
    )
    gain_one = gains[0]
    gain_two = gains[1]
    shapes = ((PATCH_COUNT, TOKEN_HIDDEN), (TOKEN_HIDDEN, PATCH_COUNT), (D, DC), (DC, D))
    totals = [jnp.zeros(shape_pair, jnp.float32) for shape_pair in shapes]
    gain_total = jnp.zeros((2, D), jnp.float32)
    results = []
    backs = []
    for micro_index in range(MICRO):
        first_row = micro_index * micro_rows
        block_in = images[first_row : first_row + micro_rows].astype(jnp.float32)
        block_cot = cotangent[first_row : first_row + micro_rows].astype(jnp.float32)
        block_keep = keep_all[first_row : first_row + micro_rows]
        forward_set = (
            lax.all_gather(low_copies[0], "fsdp", axis=0, tiled=True),
            lax.all_gather(low_copies[1], "fsdp", axis=0, tiled=True),
            lax.all_gather(low_copies[2], "fsdp", axis=0, tiled=True),
            lax.all_gather(low_copies[3], "fsdp", axis=0, tiled=True),
        )
        matmul_first = forward_set[0].reshape(PATCH_COUNT, TOKEN_HIDDEN)
        matmul_second = forward_set[1].reshape(TOKEN_HIDDEN, PATCH_COUNT)
        mat_three = forward_set[2].reshape(D, DC)
        mat_four = forward_set[3].reshape(DC, D)
        normed_one, inverse_one = normalize(block_in)
        token_input = (normed_one * gain_one).astype(jnp.bfloat16)
        token_preactivation = jnp.einsum(
            "mpw,px->mxw", token_input, matmul_first, preferred_element_type=jnp.float32
        )
        token_activation = jax.nn.gelu(token_preactivation).astype(jnp.bfloat16)
        mixed = block_in + jnp.einsum(
            "gjo,jp->gpo", token_activation, matmul_second, preferred_element_type=jnp.float32
        )
        normed_two, inverse_two = normalize(mixed)
        in_chan = (normed_two * gain_two).astype(jnp.bfloat16)
        pre_chan = jnp.einsum("bsd,df->bsf", in_chan, mat_three, preferred_element_type=jnp.float32)
        act_chan = jax.nn.gelu(pre_chan).astype(jnp.bfloat16)
        branch_chan = jnp.einsum(
            "bsf,fd->bsd", act_chan, mat_four, preferred_element_type=jnp.float32
        )
        results.append((mixed + branch_chan) * block_keep)
        behind = (
            lax.all_gather(low_copies[0], "fsdp", axis=0, tiled=True),
            lax.all_gather(low_copies[1], "fsdp", axis=0, tiled=True),
            lax.all_gather(low_copies[2], "fsdp", axis=0, tiled=True),
            lax.all_gather(low_copies[3], "fsdp", axis=0, tiled=True),
        )
        backward_first = behind[0].reshape(PATCH_COUNT, TOKEN_HIDDEN)
        backward_second = behind[1].reshape(TOKEN_HIDDEN, PATCH_COUNT)
        back_three = behind[2].reshape(D, DC)
        back_four = behind[3].reshape(DC, D)
        grad_out = block_cot * block_keep
        grad_low = grad_out.astype(jnp.bfloat16)
        totals[3] = totals[3] + jnp.einsum(
            "bsf,bsd->fd", act_chan, grad_low, preferred_element_type=jnp.float32
        )
        grad_act = jnp.einsum(
            "bsd,fd->bsf", grad_low, back_four, preferred_element_type=jnp.float32
        )
        grad_pre = gelu_back(pre_chan, grad_act).astype(jnp.bfloat16)
        totals[2] = totals[2] + jnp.einsum(
            "bsd,bsf->df", in_chan, grad_pre, preferred_element_type=jnp.float32
        )
        grad_in_chan = jnp.einsum(
            "bsf,df->bsd", grad_pre, back_three, preferred_element_type=jnp.float32
        )
        gain_grad_two = jnp.sum(grad_in_chan * normed_two, axis=(0, 1))
        grad_mixed = grad_out + norm_back(grad_in_chan * gain_two, normed_two, inverse_two)
        mixed_gradient_reduced = grad_mixed.astype(jnp.bfloat16)
        totals[1] = totals[1] + jnp.einsum(
            "afq,anq->fn",
            token_activation,
            mixed_gradient_reduced,
            preferred_element_type=jnp.float32,
        )
        grad_act_token = jnp.einsum(
            "ruo,yu->ryo",
            mixed_gradient_reduced,
            backward_second,
            preferred_element_type=jnp.float32,
        )
        token_preact_gradient = gelu_back(token_preactivation, grad_act_token).astype(jnp.bfloat16)
        totals[0] = totals[0] + jnp.einsum(
            "clz,coz->lo", token_input, token_preact_gradient, preferred_element_type=jnp.float32
        )
        grad_in_token = jnp.einsum(
            "vrx,wr->vwx", token_preact_gradient, backward_first, preferred_element_type=jnp.float32
        )
        gain_grad_one = jnp.sum(grad_in_token * normed_one, axis=(0, 1))
        gain_total = gain_total + jnp.stack([gain_grad_one, gain_grad_two])
        backs.append(grad_mixed + norm_back(grad_in_token * gain_one, normed_one, inverse_one))
    block_out = jnp.concatenate(results, axis=0)
    grad_input = jnp.concatenate(backs, axis=0)
    reduced = (
        lax.psum_scatter(totals[0].reshape(-1), "fsdp", scatter_dimension=0, tiled=True),
        lax.psum_scatter(totals[1].reshape(-1), "fsdp", scatter_dimension=0, tiled=True),
        lax.psum_scatter(totals[2].reshape(-1), "fsdp", scatter_dimension=0, tiled=True),
        lax.psum_scatter(totals[3].reshape(-1), "fsdp", scatter_dimension=0, tiled=True),
    )
    masters = (w_token_in, w_token_out, w_chan_in, w_chan_out)
    position = lax.axis_index("fsdp")
    offsets = []
    partials = []
    weight_squares = []
    for which in range(4):
        row_count, col_count = shapes[which]
        length = reduced[which].shape[0]
        offset_at = position * length
        offsets.append(offset_at)
        squares = reduced[which] * reduced[which] + 1e-30
        row_part, col_part = factor_sums(squares, offset_at, row_count, col_count)
        partials.append(row_part)
        partials.append(col_part)
        weight_squares.append(jnp.sum(masters[which] * masters[which]))
    statistics = lax.psum(
        (
            partials[0],
            partials[1],
            partials[2],
            partials[3],
            partials[4],
            partials[5],
            partials[6],
            partials[7],
            jnp.stack(weight_squares),
            gain_total,
        ),
        "fsdp",
    )
    row_edges = (
        0,
        PATCH_COUNT,
        PATCH_COUNT + TOKEN_HIDDEN,
        PATCH_COUNT + TOKEN_HIDDEN + D,
        PATCH_COUNT + TOKEN_HIDDEN + D + DC,
    )
    col_edges = (
        0,
        TOKEN_HIDDEN,
        TOKEN_HIDDEN + PATCH_COUNT,
        TOKEN_HIDDEN + PATCH_COUNT + DC,
        TOKEN_HIDDEN + PATCH_COUNT + DC + D,
    )
    rows_out = []
    cols_out = []
    raw_updates = []
    local_squares = []
    for which in range(4):
        row_count, col_count = shapes[which]
        row_new = decay_rate * row_states[row_edges[which] : row_edges[which + 1]] + (
            1.0 - decay_rate
        ) * (statistics[2 * which] / col_count)
        col_new = decay_rate * col_states[col_edges[which] : col_edges[which + 1]] + (
            1.0 - decay_rate
        ) * (statistics[2 * which + 1] / row_count)
        rows_out.append(row_new)
        cols_out.append(col_new)
        second = expand(row_new, col_new, offsets[which], reduced[which].shape[0]) / jnp.mean(
            row_new
        )
        update = reduced[which] * lax.rsqrt(second)
        raw_updates.append(update)
        local_squares.append(jnp.sum(update * update))
    update_sums = lax.psum(jnp.stack(local_squares), "fsdp")
    sizes = []
    new_weights = []
    for which in range(4):
        row_count, col_count = shapes[which]
        update_size = jnp.sqrt(update_sums[which] / (row_count * col_count))
        sizes.append(update_size)
        update = raw_updates[which] / jnp.maximum(1.0, update_size / clip_level)
        weight_scale = jnp.sqrt(statistics[8][which] / (row_count * col_count) + 1e-06)
        new_weights.append(masters[which] - step_rate * weight_scale * update)
    gain_grads = statistics[9]
    gain_stats = decay_rate * gain_states + (1.0 - decay_rate) * (gain_grads * gain_grads + 1e-30)
    gain_update = gain_grads * lax.rsqrt(gain_stats)
    gain_sizes = jnp.sqrt(jnp.mean(gain_update * gain_update, axis=1))
    gain_update = gain_update / jnp.maximum(1.0, gain_sizes / clip_level)[:, None]
    gain_scale = jnp.sqrt(jnp.mean(gains * gains, axis=1) + 1e-06)
    new_gains = gains - step_rate * gain_scale[:, None] * gain_update
    update_rms = jnp.concatenate([jnp.stack(sizes), gain_sizes])
    return (
        block_out,
        grad_input,
        reduced[0],
        reduced[1],
        reduced[2],
        reduced[3],
        new_weights[0],
        new_weights[1],
        new_weights[2],
        new_weights[3],
        gain_grads,
        gain_stats,
        new_gains,
        jnp.concatenate(rows_out),
        jnp.concatenate(cols_out),
        update_rms,
    )


def solution(mesh):
    in_specs = (
        P("fsdp", None, None),
        P("fsdp", None, None),
        P("fsdp"),
        P("fsdp"),
        P("fsdp"),
        P("fsdp"),
        P("fsdp"),
        P(),
        P(),
        P(),
        P(),
    )
    out_specs = (
        P("fsdp", None, None),
        P("fsdp", None, None),
        P("fsdp"),
        P("fsdp"),
        P("fsdp"),
        P("fsdp"),
        P("fsdp"),
        P("fsdp"),
        P("fsdp"),
        P("fsdp"),
        P(),
        P(),
        P(),
        P(),
        P(),
        P(),
    )
    return jax.shard_map(shards, mesh=mesh, in_specs=in_specs, out_specs=out_specs, check_vma=False)
```

profile of v0, /device:TPU:0, one launch (start us, length us, event | category | flops | bytes accessed | tf_op | source)
XLA Modules:
  0.0 841.7 jit_solution(2607171227867735593)
XLA Ops:
  7.2 1.4 multiply_reduce_fusion.15
  8.6 1.4 multiply_reduce_fusion.14
  11.4 2.3 multiply_reduce_fusion.11
  13.8 2.4 multiply_reduce_fusion.10
  17.0 0.8 slice_reduce_fusion
  17.8 3.3 fusion.108
  22.6 1.1 copy-done.21
  23.7 2.2 fusion.107
  25.9 116.9 %all-reduce.19.cloned.1.call-done = (bf16[75264]{0:T(1024)(128)(2,1)}, bf16[75264]{0:T(1024)(128)(2,1)}) async-done(((bf16[75264]{0:T(1024)(128)(2,1)}, bf16[75264]{0:T(1024)(128)(2,1)}), (bf16[75264]{0:T(1024)(128)(2,1)}, bf16[75264]{0:T(1024)(128)(2,1)})) %all-reduce.19.cloned.1.call-update) | async-done | bytes 301072
  142.8 1.5 reshape.254
  144.4 1.0 reshape.269
  145.4 1.5 fusion.73
  146.9 2.5 fusion.112
  149.9 1.5 fusion.70
  151.5 2.3 fusion.113
  153.9 1.4 copy-done.9
  155.7 55.7 %all-gather.3.cloned.1.call-done = bf16[2359296]{0:T(1024)(128)(2,1)} async-done(((bf16[73728]{0:T(1024)(128)(2,1)}), bf16[2359296]{0:T(1024)(128)(2,1)}) %all-gather.3.cloned.1.call-update) | async-done | bytes 4718608 | tf_op jit(solution)/shard_map/all_gather | solution.py:96
  211.4 8.2 reshape.271
  219.6 6.3 fusion.93
  225.9 3.8 copy-done.50
  229.6 9.4 %fusion.79 = f32[3072,768,1]{1,0,2:T(8,128)} fusion(f32[4]{0:T(128)S(1)} %get-tuple-element.161, bf16[4,196,768]{2,0,1:T(4,128)(2,1)S(1)} %copy-done.23, f32[4,196,3072]{2,1,0:T(8,128)S(1)} %fusion.93), kind=kOutput, calls=%fused_computation.125 | convolution fusion | flops 3722858496 | bytes 20275216 | tf_op jit(solution)/shard_map/bsf,bsd->fd/dot_general | solution.py:132
  239.1 38.7 %all-gather.5.cloned.1.call-done = bf16[2359296]{0:T(1024)(128)(2,1)} async-done(((bf16[73728]{0:T(1024)(128)(2,1)}), bf16[2359296]{0:T(1024)(128)(2,1)}) %all-gather.5.cloned.1.call-update) | async-done | bytes 4718608 | tf_op jit(solution)/shard_map/all_gather | solution.py:97
  277.8 9.2 %reshape.272 = bf16[3072,768,1]{1,0,2:T(8,128)(2,1)} reshape(bf16[2359296]{0:T(1024)(128)(2,1)} %all-gather.5.cloned.1.call-done) | data formatting | bytes 9437184 | tf_op jit(solution)/shard_map/reshape | solution.py:102
  287.0 12.6 %fusion.6 = bf16[4,196,3072]{2,1,0:T(8,128)(2,1)S(1)} fusion(f32[4,196,3072]{2,1,0:T(8,128)} %copy-done.50, bf16[3072,768,1]{1,0,2:T(8,128)(2,1)} %reshape.272, f32[4]{0:T(128)S(1)} %get-tuple-element.161, bf16[4,196,768]{2,0,1:T(4,128)(2,1)} %get-tuple-element.137), kind=kOutput, calls=%fused_computation.10 | convolution fusion | flops 3749351424 | bytes 20373520 | tf_op jit(solution)/shard_map/bsd,fd->bsf/dot_general | solution.py:135
  299.6 8.3 multiply_reduce_fusion.1
  307.9 7.9 fusion.92
  315.9 9.1 %fusion.94 = f32[4,196,3072]{2,1,0:T(8,128)} fusion(bf16[768,3072,1]{1,0,2:T(8,128)(2,1)} %reshape.271, f32[4,196,768]{2,1,0:T(8,128)S(1)} %copy-done.7, f32[4,196]{1,0:T(4,128)S(1)} %add_rsqrt_fusion, f32[4,196]{1,0:T(4,128)S(1)} %broadcast_multiply_fusion.12, f32[768]{0:T(1024)S(1)} %get-tuple-element.100), kind=kOutput, calls=%fused_computation.147 | convolution fusion | flops 3701784576 | bytes 16770176 | tf_op jit(solution)/shard_map/bsd,df->bsf/dot_general | solution.py:114
  325.0 12.9 %fusion.13 = bf16[4,196,3072]{2,1,0:T(8,128)(2,1)} fusion(f32[4,196,3072]{2,1,0:T(8,128)} %fusion.94, bf16[3072,768,1]{1,0,2:T(8,128)(2,1)S(1)} %bitcast.166, f32[4]{0:T(128)S(1)} %get-tuple-element.162, bf16[4,196,768]{2,0,1:T(4,128)(2,1)S(1)} %copy-done.12), kind=kOutput, calls=%fused_computation.17 | convolution fusion | flops 3749351424 | bytes 20373520 | tf_op jit(solution)/shard_map/bsd,fd->bsf/dot_general | solution.py:135
  337.9 9.7 %multiply_reduce_fusion = (f32[768]{0:T(1024)S(1)}, f32[4,196]{1,0:T(4,128)S(1)}, f32[4,196]{1,0:T(4,128)S(1)}, f32[4,196,768]{2,1,0:T(8,128)}, f32[4,196,768]{2,1,0:T(8,128)S(1)}) fusion(f32[4,196,768]{2,1,0:T(8,128)S(1)} %copy-done.7, f32[4,196]{1,0:T(4,128)S(1)} %add_rsqrt_fusion, f32[4,196]{1,0:T(4,128)S(1)} %broadcast_multiply_fusion.12, ...), kind=kOutput, calls=%fused_computation.91 | convolution fusion | flops 3710211840 | bytes 22813200 | tf_op jit(solution)/shard_map/bsf,df->bsd/dot_general | solution.py:142
  347.6 1.0 multiply_add_fusion
  348.6 1.9 convolution_bitcast_fusion
  350.5 5.0 fusion.28
  355.5 13.4 %bitcast_add_fusion = f32[3072,768]{1,0:T(8,128)} fusion(f32[3072,768,1]{1,0,2:T(8,128)} %fusion.79, f32[4]{0:T(128)S(1)} %get-tuple-element.162, bf16[4,196,768]{2,0,1:T(4,128)(2,1)S(1)} %copy-done.12, f32[4,196,3072]{2,1,0:T(8,128)} %fusion.94), kind=kOutput, calls=%fused_computation.20 | convolution fusion | flops 3725217792 | bytes 29712400 | tf_op jit(solution)/shard_map/bsf,bsd->fd/dot_general | solution.py:132
  368.8 10.7 %reshape.260 = f32[2359296]{0:T(1024)} reshape(f32[3072,768]{1,0:T(8,128)} %bitcast_add_fusion) | data formatting | bytes 18874368 | tf_op jit(solution)/shard_map/reshape | solution.py:176
  379.6 9.7 %fusion.14 = f32[96,24,8,128]{3,2,1,0:T(8,128)S(1)} fusion(f32[768,3072,1]{1,0,2:T(8,128)} %fusion.92, bf16[4,196,3072]{2,1,0:T(8,128)(2,1)} %fusion.13, f32[4,196,768]{2,1,0:T(8,128)S(1)} %copy-done.7, f32[4,196]{1,0:T(4,128)S(1)} %add_rsqrt_fusion, f32[4,196]{1,0:T(4,128)S(1)} %broadcast_multiply_fusion.12, f32[768]{0:T(1024)S(1)} %get-tuple-element.100), kind=kOutput, calls=%fused_computation.22 | convolution fusion | flops 3704143872 | bytes 26109056 | tf_op jit(solution)/shard_map/bsd,bsf->df/dot_general | solution.py:139
  389.3 5.9 copy.118
  395.2 7.0 fusion.21
  402.2 1.9 fusion.68
  404.3 1.1 reshape.258
  405.4 2.7 convolution_bitcast_fusion.2
  408.2 1.0 fusion.67
  409.2 0.7 reshape.257
  410.1 2.7 pad_maximum_fusion.2
  412.9 11.8 %add_multiply_fusion.1 = f32[4,196,768]{2,1,0:T(8,128)S(1)} fusion(f32[4,196,768]{2,1,0:T(8,128)} %copy-done.9, bf16[3072,768,1]{1,0,2:T(8,128)(2,1)} %reshape.272, f32[4]{0:T(128)S(1)} %get-tuple-element.161, f32[4,196,3072]{2,1,0:T(8,128)} %copy-done.50), kind=kOutput, calls=%fused_computation.104 | convolution fusion | flops 3722256384 | bytes 19169296 | tf_op jit(solution)/shard_map/bsf,fd->bsd/dot_general | solution.py:116
  424.7 10.0 %add_multiply_fusion = f32[4,196,768]{2,1,0:T(8,128)S(1)} fusion(f32[4,196,768]{2,1,0:T(8,128)S(1)} %copy-done.8, bf16[3072,768,1]{1,0,2:T(8,128)(2,1)} %reshape.272, f32[4]{0:T(128)S(1)} %get-tuple-element.162, f32[4,196,3072]{2,1,0:T(8,128)} %fusion.94), kind=kOutput, calls=%fused_computation.101 | convolution fusion | flops 3722256384 | bytes 19169296 | tf_op jit(solution)/shard_map/bsf,fd->bsd/dot_general | solution.py:116
  435.1 3.7 copy.96
  438.8 2.1 fusion.61
  441.3 2.8 fusion.54
  444.1 1.0 fusion.53
  445.5 3.7 copy.97
  449.2 274.9 %all-reduce.17.cloned.1.call-done = (f32[75264]{0:T(1024)}, f32[75264]{0:T(1024)}, f32[2359296]{0:T(1024)}, f32[2359296]{0:T(1024)}) async-done(((f32[75264]{0:T(1024)}, f32[75264]{0:T(1024)}, f32[2359296]{0:T(1024)}, f32[2359296]{0:T(1024)}), (f32[75264]{0:T(1024)}, f32[75264]{0:T(1024)}, f32[2359296]{0:T(1024)}, f32[2359296]{0:T(1024)})) %all-reduce.17.cloned.1.call-update) | async-done | bytes 19476496
  724.1 0.9 add_dynamic-update-slice_fusion.3
  725.1 0.9 add_dynamic-update-slice_fusion.2
  726.3 1.3 add_dynamic-update-slice_fusion
  728.1 1.3 add_dynamic-update-slice_fusion.1
  730.4 40.4 %all-reduce.11 = (f32[3072]{0:T(1024)S(1)}, f32[768]{0:T(1024)S(1)}, f32[768]{0:T(1024)S(1)}, f32[3072]{0:T(1024)S(1)}, f32[384]{0:T(512)S(1)}, /*index=5*/f32[196]{0:T(256)S(1)}, f32[196]{0:T(256)S(1)}, f32[384]{0:T(512)S(1)}) all-reduce(f32[3072]{0:T(1024)S(1)} %slice.114, ...), channel_id=1, replica_groups=mesh['fsdp'=32] {'fsdp'}, use_global_device_ids=true, to_apply=%region_44.45 | all-reduce | flops 8840 | bytes 70720 | tf_op jit(solution)/shard_map/psum | solution.py:193
  777.7 0.7 multiply_reduce_fusion.13
  779.1 0.8 multiply_reduce_fusion.8
  779.9 0.8 multiply_reduce_fusion.9
  780.6 2.7 pad_maximum_fusion.3
  783.9 39.5 %all-reduce.10 = (f32[4]{0:T(128)S(1)}, f32[4]{0:T(128)S(1)}, f32[2,768]{1,0:T(2,128)S(1)}) all-reduce(f32[4]{0:T(128)S(1)} %pad_maximum_fusion.3, f32[4]{0:T(128)S(1)} %pad_maximum_fusion.2, f32[2,768]{1,0:T(2,128)S(1)} %maximum_add_fusion), channel_id=1, replica_groups=mesh['fsdp'=32] {'fsdp'}, use_global_device_ids=true, to_apply=%region_49.50 | all-reduce | flops 1544 | bytes 12352 | tf_op jit(solution)/shard_map/psum | solution.py:242
  831.0 0.9 multiply_subtract_fusion.1
  831.8 0.9 multiply_subtract_fusion
  833.4 0.7 multiply_subtract_fusion.3
  (215 shorter events, 16.2 us)
Async XLA Ops:
  7.2 135.7 %all-reduce.19.cloned.1.call-start = ((), (), s32[]{:S(2)}) async-start(), calls=%async_computation.3 | async-start | bytes 606208
  10.3 0.7 copy-start.27
  10.7 0.7 copy-start.26
  11.4 200.0 %all-gather.3.cloned.1.call-start = ((), (), s32[]{:S(2)}) async-start(), calls=%async_computation | async-start | bytes 4866048 | tf_op jit(solution)/shard_map/all_gather | solution.py:96
  13.8 264.0 %all-gather.5.cloned.1.call-start = ((), (), s32[]{:S(2)}) async-start(), calls=%async_computation.1 | async-start | bytes 4866048 | tf_op jit(solution)/shard_map/all_gather | solution.py:97
  16.3 707.8 %all-reduce.17.cloned.1.call-start = ((), (), s32[]{:S(2)}) async-start(), calls=%async_computation.2 | async-start | bytes 38961152
  17.8 132.2 %copy-start.32 = (f32[768]{0:T(1024)}, f32[768]{0:T(1024)S(1)}, u32[]{:S(2)}) copy-start(f32[768]{0:T(1024)S(1)} %get-tuple-element.101) | copy-start | bytes 9220
  21.1 125.8 %copy-start = (bf16[4,196,768]{2,0,1:T(4,128)(2,1)}, bf16[4,196,768]{2,0,1:T(4,128)(2,1)S(1)}, u32[]{:S(2)}) copy-start(bf16[4,196,768]{2,0,1:T(4,128)(2,1)S(1)} %get-tuple-element.140) | copy-start | bytes 3612676
  21.1 130.4 %copy-start.2 = (bf16[4,196,768]{2,0,1:T(4,128)(2,1)}, bf16[4,196,768]{2,0,1:T(4,128)(2,1)S(1)}, u32[]{:S(2)}) copy-start(bf16[4,196,768]{2,0,1:T(4,128)(2,1)S(1)} %get-tuple-element.139) | copy-start | bytes 3612676
  21.1 2.6 copy-start.21
  21.5 128.4 %copy-start.36 = (f32[4,196]{1,0:T(4,128)}, f32[4,196]{1,0:T(4,128)S(1)}, u32[]{:S(2)}) copy-start(f32[4,196]{1,0:T(4,128)S(1)} %broadcast_multiply_fusion.15) | copy-start | bytes 9412
  22.1 123.3 %copy-start.30 = (f32[4,196]{1,0:T(4,128)}, f32[4,196]{1,0:T(4,128)S(1)}, u32[]{:S(2)}) copy-start(f32[4,196]{1,0:T(4,128)S(1)} %broadcast_multiply_fusion.13) | copy-start | bytes 9412
  22.6 127.3 %copy-start.41 = (f32[4,196]{1,0:T(4,128)}, f32[4,196]{1,0:T(4,128)S(1)}, u32[]{:S(2)}) copy-start(f32[4,196]{1,0:T(4,128)S(1)} %add_rsqrt_fusion.3) | copy-start | bytes 9412
  23.7 121.7 %copy-start.34 = (f32[4,196]{1,0:T(4,128)}, f32[4,196]{1,0:T(4,128)S(1)}, u32[]{:S(2)}) copy-start(f32[4,196]{1,0:T(4,128)S(1)} %add_rsqrt_fusion.1) | copy-start | bytes 9412
  145.4 4.6 copy-start.19
  146.9 2.5 copy-start.14
  149.4 2.0 copy-start.6
  151.5 2.3 copy-start.13
  153.8 1.4 copy-start.9
  155.7 63.9 %copy-start.10 = (f32[4,196,768]{2,1,0:T(8,128)S(1)}, f32[4,196,768]{2,1,0:T(8,128)}, u32[]{:S(2)}) copy-start(f32[4,196,768]{2,1,0:T(8,128)} %copy-done.9) | copy-start | bytes 7225348
  219.6 10.1 %copy-start.23 = (bf16[4,196,768]{2,0,1:T(4,128)(2,1)S(1)}, bf16[4,196,768]{2,0,1:T(4,128)(2,1)}, u32[]{:S(2)}) copy-start(bf16[4,196,768]{2,0,1:T(4,128)(2,1)} %get-tuple-element.137) | copy-start | bytes 3612676
  225.8 3.8 copy-start.50
  299.6 8.3 copy-start.11
  307.9 7.9 copy-start.7
  307.9 17.0 %slice-start = ((s8[4718592]{0:T(1024)(128)(4,1)}), s8[524288]{0:T(1024)(128)(4,1)S(1)}, s32[]{:S(2)}) async-start(s8[4718592]{0:T(1024)(128)(4,1)} %bitcast.165), calls=%async_computation.4 | async-start | bytes 1048576
  315.8 9.1 %copy-start.12 = (bf16[4,196,768]{2,0,1:T(4,128)(2,1)S(1)}, bf16[4,196,768]{2,0,1:T(4,128)(2,1)}, u32[]{:S(2)}) copy-start(bf16[4,196,768]{2,0,1:T(4,128)(2,1)} %get-tuple-element.138) | copy-start | bytes 3612676
  315.8 9.1 %slice-start.1 = ((s8[4718592]{0:T(1024)(128)(4,1)}), s8[4194304]{0:T(1024)(128)(4,1)S(1)}, s32[]{:S(2)}) async-start(s8[4718592]{0:T(1024)(128)(4,1)} %bitcast.165), calls=%async_computation.5 | async-start | bytes 8388608
  315.8 22.0 %slice-start.6 = ((s8[4718592]{0:T(1024)(128)(4,1)}), s8[4194304]{0:T(1024)(128)(4,1)S(1)}, s32[]{:S(2)}) async-start(s8[4718592]{0:T(1024)(128)(4,1)} %bitcast.171), calls=%async_computation.10 | async-start | bytes 8388608
  315.9 32.7 %slice-start.4 = ((s8[4718592]{0:T(1024)(128)(4,1)}), s8[4194304]{0:T(1024)(128)(4,1)S(1)}, s32[]{:S(2)}) async-start(s8[4718592]{0:T(1024)(128)(4,1)} %bitcast.169), calls=%async_computation.8 | async-start | bytes 8388608
  324.9 12.9 %slice-start.7 = ((s8[4718592]{0:T(1024)(128)(4,1)}), s8[524288]{0:T(1024)(128)(4,1)S(1)}, s32[]{:S(2)}) async-start(s8[4718592]{0:T(1024)(128)(4,1)} %bitcast.171), calls=%async_computation.11 | async-start | bytes 1048576
  324.9 23.7 %slice-start.5 = ((s8[4718592]{0:T(1024)(128)(4,1)}), s8[524288]{0:T(1024)(128)(4,1)S(1)}, s32[]{:S(2)}) async-start(s8[4718592]{0:T(1024)(128)(4,1)} %bitcast.169), calls=%async_computation.9 | async-start | bytes 1048576
  348.6 1.9 copy-start.4
  389.3 5.9 copy-start.17
  389.3 12.9 %slice-start.2 = ((s8[4718592]{0:T(1024)(128)(4,1)}), s8[524288]{0:T(1024)(128)(4,1)S(1)}, s32[]{:S(2)}) async-start(s8[4718592]{0:T(1024)(128)(4,1)} %bitcast.167), calls=%async_computation.6 | async-start | bytes 1048576
  395.2 7.0 slice-start.3
  402.2 3.2 copy-start.1
  402.2 3.2 copy-start.31
  402.2 3.2 copy-start.33
  402.2 3.2 copy-start.35
  405.4 2.8 copy-start.3
  405.4 2.8 copy-start.37
  405.4 2.8 copy-start.42
  405.4 2.8 copy-start.48
  409.9 2.8 copy-start.38
  412.9 11.8 %copy-start.8 = (f32[4,196,768]{2,1,0:T(8,128)S(1)}, f32[4,196,768]{2,1,0:T(8,128)}, u32[]{:S(2)}) copy-start(f32[4,196,768]{2,1,0:T(8,128)} %copy-done.6) | copy-start | bytes 7225348
  435.1 3.7 copy-start.20
  435.1 3.7 copy-start.49
  438.8 2.1 copy-start.18
  438.8 2.5 copy-start.22
  441.3 2.8 copy-start.5
  449.2 321.6 %copy-start.45 = (f32[4420]{0:T(1024)S(1)}, f32[4420]{0:T(1024)}, u32[]{:S(2)}) copy-start(f32[4420]{0:T(1024)} %param.19) | copy-start | bytes 53044
  724.1 50.3 %copy-start.46 = (f32[4420]{0:T(1024)S(1)}, f32[4420]{0:T(1024)}, u32[]{:S(2)}) copy-start(f32[4420]{0:T(1024)} %param.20) | copy-start | bytes 53044
  725.0 108.4 %copy-start.28 = (f32[2352]{0:T(1024)}, f32[2352]{0:T(1024)S(1)}, u32[]{:S(2)}) copy-start(f32[2352]{0:T(1024)S(1)} %get-tuple-element.130) | copy-start | bytes 28228
  726.1 106.7 %copy-start.29 = (f32[2352]{0:T(1024)}, f32[2352]{0:T(1024)S(1)}, u32[]{:S(2)}) copy-start(f32[2352]{0:T(1024)S(1)} %get-tuple-element.132) | copy-start | bytes 28228
  727.6 104.2 %copy-start.15 = (f32[73728]{0:T(1024)}, f32[73728]{0:T(1024)S(1)}, u32[]{:S(2)}) copy-start(f32[73728]{0:T(1024)S(1)} %get-tuple-element.136) | copy-start | bytes 884740
  729.5 101.5 %copy-start.16 = (f32[73728]{0:T(1024)}, f32[73728]{0:T(1024)S(1)}, u32[]{:S(2)}) copy-start(f32[73728]{0:T(1024)S(1)} %get-tuple-element.134) | copy-start | bytes 884740
  729.5 100.7 %copy-start.47 = (f32[2,768]{1,0:T(2,128)S(1)}, f32[2,768]{1,0:T(2,128)}, u32[]{:S(2)}) copy-start(f32[2,768]{1,0:T(2,128)} %param.21) | copy-start | bytes 18436
  729.5 101.5 %copy-start.24 = (f32[73728]{0:T(1024)S(1)}, f32[73728]{0:T(1024)}, u32[]{:S(2)}) copy-start(f32[73728]{0:T(1024)} %param.16) | copy-start | bytes 884740
  771.5 60.3 %copy-start.25 = (f32[73728]{0:T(1024)S(1)}, f32[73728]{0:T(1024)}, u32[]{:S(2)}) copy-start(f32[73728]{0:T(1024)} %param.17) | copy-start | bytes 884740
  774.9 57.8 %copy-start.39 = (f32[2352]{0:T(1024)S(1)}, f32[2352]{0:T(1024)}, u32[]{:S(2)}) copy-start(f32[2352]{0:T(1024)} %param.15) | copy-start | bytes 28228
  775.0 58.5 %copy-start.40 = (f32[2352]{0:T(1024)S(1)}, f32[2352]{0:T(1024)}, u32[]{:S(2)}) copy-start(f32[2352]{0:T(1024)} %param.14) | copy-start | bytes 28228
  823.5 11.3 %copy-start.43 = (f32[2,768]{1,0:T(2,128)}, f32[2,768]{1,0:T(2,128)S(1)}, u32[]{:S(2)}) copy-start(f32[2,768]{1,0:T(2,128)S(1)} %get-tuple-element.104) | copy-start | bytes 18436
  830.3 4.4 copy-start.44
Sparse Core Ops, SparseCore 0:
  14.0 128.7 all-reduce.18
  146.7 64.5 all-gather.2
  215.3 62.4 all-gather.4
  410.1 313.9 all-reduce.16
where the time goes:
time: 848 us; the launch traced here: 842 us
  waiting for transfers between devices  486 us (57%)
  matrix products  153 us (18%)
  blocking collectives  79.9 us (9%)
  local copies, waits for them, and re-layouts  65.3 us (8%)
  other arithmetic  32.9 us (4%)
  between operations  24.2 us (3%)
    unnamed x6, waiting for transfers between devices  392 us
    all_gather x1, waiting for transfers between devices, shards(): lax.all_gather(low_copies[2], 'fsdp', axis=0, tiled=True)  55.7 us
    psum x1, blocking collectives, shards(): lax.psum((partials[0], partials[1], partials[2], partials[3], partials[4]...  40.4 us
    psum x1, blocking collectives, shards(): update_sums = lax.psum(jnp.stack(local_squares), 'fsdp')  39.5 us
    all_gather x1, waiting for transfers between devices, shards(): lax.all_gather(low_copies[3], 'fsdp', axis=0, tiled=True)  38.7 us
    dot_general x2, matrix products, shards(): jnp.einsum('bsd,fd->bsf', grad_low, back_four, preferred_element_type=jnp...  25.6 us
    dot_general x2, matrix products, shards(): jnp.einsum('bsf,bsd->fd', act_chan, grad_low, preferred_element_type=jnp....  22.8 us
    dot_general x2, matrix products, shards(): jnp.einsum('bsf,fd->bsd', act_chan, mat_four, preferred_element_type=jnp....  21.8 us
  transfers between devices with their start and end apart: 4, of which 4 were waited for; matrix products, arithmetic and copies ran while one was open for 10% of the time, Pallas kernels for 0%

commit v1 on v0

v1 whole, which is shorter than its diff:
```python
import functools

import jax
import jax.numpy as jnp
from jax import lax
from jax.experimental import pallas as pl
from jax.experimental.pallas import tpu as pltpu
from jax.sharding import PartitionSpec as P

D = 768
PATCHES = 196
HIDDEN = 384
DC = 3072
PAD = 208
UNITS = 2
F = DC // (2 * UNITS)
BLOCKS = 16
TILE = D // BLOCKS
GROUP = 2

DECAY = 0.5
CLIP = 0.5
STEP = 1.0

NN = ((1,), (0,))
NT = ((1,), (1,))
TN = ((0,), (0,))

GELU_A = 0.7978845608028654
GELU_B = 0.7978845608028654 * 0.044715

BF = jnp.bfloat16
F32 = jnp.float32


def dot(a, b, dims):
    return lax.dot_general(a, b, (dims, ((), ())), preferred_element_type=F32)


def gelu_pair(v):
    square = v * v
    t = jnp.tanh(v * (GELU_A + GELU_B * square))
    half = 0.5 + 0.5 * t
    slope = half + (0.5 * v) * (1.0 - t * t) * (GELU_A + (3.0 * GELU_B) * square)
    return v * half, slope


def normalize(values):
    centred = values - jnp.mean(values, axis=-1, keepdims=True)
    spread = jnp.mean(centred * centred, axis=-1, keepdims=True)
    inverse = lax.rsqrt(spread + 1e-06)
    return centred * inverse, inverse


def norm_back(grad, normed, inverse):
    first = jnp.mean(grad, axis=-1, keepdims=True)
    second = jnp.mean(grad * normed, axis=-1, keepdims=True)
    return inverse * (grad - first - normed * second)


def params(mib=56):
    return pltpu.CompilerParams(vmem_limit_bytes=mib * 2**20)


ANY = pl.BlockSpec(memory_space=pl.ANY)
SMEM = pl.BlockSpec(memory_space=pltpu.SMEM)


def whole(shape):
    return pl.BlockSpec(shape, lambda *_: (0,) * len(shape))


def image(rows):
    return pl.BlockSpec((1, rows, D), lambda i: (i, 0, 0))


def struct(shape, dtype):
    return jax.ShapeDtypeStruct(shape, dtype)


def first_kernel(counts, x, cot, gains, y1, dout):
    normed, _ = normalize(x[0].astype(F32))
    y1[0] = (normed * gains[0:1, :]).astype(BF)
    keep = (pl.program_id(0) < counts[0]).astype(F32)
    dout[0, :PATCHES, :] = (cot[0].astype(F32) * keep).astype(BF)
    dout[0, PATCHES:, :] = jnp.zeros((PAD - PATCHES, D), BF)


def first_norm(counts, images, cotangent, gains):
    count = images.shape[0]
    return pl.pallas_call(
        first_kernel,
        grid=(count,),
        in_specs=[SMEM, image(PATCHES), image(PATCHES), whole((2, D))],
        out_specs=[image(PATCHES), image(PAD)],
        out_shape=[struct((count, PATCHES, D), BF), struct((count, PAD, D), BF)],
        compiler_params=params(),
        name="first_norm",
    )(counts, images, cotangent, gains)


def token_kernel(x, y1, w1, w2, gains, h, slope, x1, y2):
    act, der = gelu_pair(dot(w1[...], y1[0], TN))
    act = act.astype(BF)
    h[0] = act
    slope[0] = der.astype(BF)
    mixed = x[0].astype(F32) + dot(w2[...], act, TN)
    x1[0] = mixed
    normed, _ = normalize(mixed)
    y2[0, :PATCHES, :] = (normed * gains[1:2, :]).astype(BF)
    y2[0, PATCHES:, :] = jnp.zeros((PAD - PATCHES, D), BF)


def token_forward(images, y1, w1, w2, gains):
    count = images.shape[0]
    return pl.pallas_call(
        token_kernel,
        grid=(count,),
        in_specs=[
            image(PATCHES),
            image(PATCHES),
            whole((PATCHES, HIDDEN)),
            whole((HIDDEN, PATCHES)),
            whole((2, D)),
        ],
        out_specs=[image(HIDDEN), image(HIDDEN), image(PATCHES), image(PAD)],
        out_shape=[
            struct((count, HIDDEN, D), BF),
            struct((count, HIDDEN, D), BF),
            struct((count, PATCHES, D), F32),
            struct((count, PAD, D), BF),
        ],
        compiler_params=params(),
        name="token_forward",
    )(images, y1, w1, w2, gains)


def load_unit(table, pieces, unit, dest, sems):
    copies = []
    for at in range(BLOCKS):
        source = pieces[at * 2 // BLOCKS].at[at % (BLOCKS // 2), unit]
        row = pl.multiple_of(table[at] * TILE, 16)
        copies.append(pltpu.make_async_copy(source, dest.at[pl.ds(row, TILE), :], sems.at[at]))
    return copies


def channel_kernel(unit, forward, table, lo, hi, left, right, *refs):
    if forward:
        out, slope, grad, weight, kept, other, sems, other_sem = refs
    else:
        slope, out, grad, weight, kept, other, sems, other_sem = refs
    step = pl.program_id(0)
    rows = left.shape[0]
    other_copy = pltpu.make_async_copy(right, other, other_sem)

    @pl.when(step == 0)
    def _():
        copies = load_unit(table, (lo, hi), unit, weight, sems)
        for copy in copies:
            copy.start()
        other_copy.start()
        for copy in copies:
            copy.wait()

    here = pl.ds(pl.multiple_of(step * rows, 16), rows)
    if forward:
        act, der = gelu_pair(dot(left[...], weight[...], NN))
        act = act.astype(BF)
        slope[...] = der.astype(BF)
    else:
        act = (slope[...].astype(F32) * dot(left[...], weight[...], NT)).astype(BF)
    out[...] = act
    kept[here, :] = act

    @pl.when(step == pl.num_programs(0) - 1)
    def _():
        other_copy.wait()
        if forward:
            total = dot(kept[...], other[...], TN)
        else:
            total = dot(other[...], kept[...], TN)
        total = total.astype(BF)
        for at in range(BLOCKS):
            grad[table[BLOCKS + at]] = total[at * TILE : (at + 1) * TILE, :]


def channel_unit(forward, unit, table, pieces, left, right, slope=None):
    rows = left.shape[0]
    tile = GROUP * PAD
    tiles = pl.BlockSpec((tile, D), lambda i: (i, 0))
    acts = pl.BlockSpec((tile, F), lambda i: (i, 0))
    grad = whole((BLOCKS, TILE, D))
    operands = [table, pieces[0], pieces[1], left, right]
    in_specs = [SMEM, ANY, ANY, tiles, ANY]
    if forward:
        out_specs = [acts, acts, grad]
        out_shape = [struct((rows, F), BF)] * 2 + [struct((BLOCKS, TILE, D), BF)]
    else:
        operands.append(slope)
        in_specs.append(acts)
        out_specs = [acts, grad]
        out_shape = [struct((rows, F), BF), struct((BLOCKS, TILE, D), BF)]
    return pl.pallas_call(
        functools.partial(channel_kernel, unit, forward),
        grid=(rows // tile,),
        in_specs=in_specs,
        out_specs=out_specs,
        out_shape=out_shape,
        scratch_shapes=[
            pltpu.VMEM((D, F), BF),
            pltpu.VMEM((rows, F), BF),
            pltpu.VMEM((rows, D), BF),
            pltpu.SemaphoreType.DMA((BLOCKS,)),
            pltpu.SemaphoreType.DMA,
        ],
        compiler_params=params(),
        cost_estimate=pl.CostEstimate(
            flops=4 * rows * D * F, bytes_accessed=12 * 2**20, transcendentals=rows * F
        ),
        name="channel_forward" if forward else "channel_backward",
    )(*operands)


def back_kernel(own_table, other_table, *refs):
    pieces = refs[0:4]
    d0, d1, d2, d3, dout, x1, h, slope, y1, w2, gains = refs[4:15]
    dx1, da, g1, g2, dg2, weights, sems = refs[15:]
    step = pl.program_id(0)

    @pl.when(step == 0)
    def _():
        copies = []
        for at in range(2 * UNITS):
            table = own_table if at < UNITS else other_table
            pair = pieces[0:2] if at < UNITS else pieces[2:4]
            copies += load_unit(table, pair, at % UNITS, weights.at[at], sems.at[at])
        for copy in copies:
            copy.start()
        for copy in copies:
            copy.wait()
        g1[...] = jnp.zeros_like(g1)
        g2[...] = jnp.zeros_like(g2)
        dg2[...] = jnp.zeros_like(dg2)

    dy2 = dot(d0[...], weights[0], NT)
    dy2 += dot(d1[...], weights[1], NT)
    dy2 += dot(d2[...], weights[2], NT)
    dy2 += dot(d3[...], weights[3], NT)
    for at in range(GROUP):
        grad = dy2[at * PAD : at * PAD + PATCHES, :]
        normed, inverse = normalize(x1[at])
        dg2[...] += jnp.sum(grad * normed, axis=0, keepdims=True)
        total = dout[at, :PATCHES, :].astype(F32) + norm_back(
            grad * gains[1:2, :], normed, inverse
        )
        dx1[at] = total
        low = total.astype(BF)
        g2[...] += dot(h[at], low, NT)
        back = (slope[at].astype(F32) * dot(w2[...], low, NN)).astype(BF)
        da[at] = back
        g1[...] += dot(y1[at], back, NT)


def backward(tables, pieces, dcs, dout, x1, h, slope, y1, w2, gains):
    count = x1.shape[0]
    tile = GROUP * PAD

    def images(rows):
        return pl.BlockSpec((GROUP, rows, D), lambda i: (i, 0, 0))

    acts = pl.BlockSpec((tile, F), lambda i: (i, 0))
    return pl.pallas_call(
        back_kernel,
        grid=(count // GROUP,),
        in_specs=[SMEM, SMEM]
        + [ANY] * 4
        + [acts] * 4
        + [
            images(PAD),
            images(PATCHES),
            images(HIDDEN),
            images(HIDDEN),
            images(PATCHES),
            whole((HIDDEN, PATCHES)),
            whole((2, D)),
        ],
        out_specs=[
            images(PATCHES),
            images(HIDDEN),
            whole((PATCHES, HIDDEN)),
            whole((HIDDEN, PATCHES)),
            whole((1, D)),
        ],
        out_shape=[
            struct((count, PATCHES, D), F32),
            struct((count, HIDDEN, D), BF),
            struct((PATCHES, HIDDEN), F32),
            struct((HIDDEN, PATCHES), F32),
            struct((1, D), F32),
        ],
        scratch_shapes=[
            pltpu.VMEM((2 * UNITS, D, F), BF),
            pltpu.SemaphoreType.DMA((2 * UNITS, BLOCKS)),
        ],
        compiler_params=params(),
        cost_estimate=pl.CostEstimate(
            flops=2 * count * PAD * D * DC, bytes_accessed=40 * 2**20, transcendentals=0
        ),
        name="backward",
    )(*tables, *pieces, *dcs, dout, x1, h, slope, y1, w2, gains)


def input_kernel(x, da, dx1, w1, gains, out, dg1):
    @pl.when(pl.program_id(0) == 0)
    def _():
        dg1[...] = jnp.zeros_like(dg1)

    grad = dot(w1[...], da[0], NN)
    normed, inverse = normalize(x[0].astype(F32))
    dg1[...] += jnp.sum(grad * normed, axis=0, keepdims=True)
    out[0] = dx1[0] + norm_back(grad * gains[0:1, :], normed, inverse)


def input_gradient(images, da, dx1, w1, gains):
    count = images.shape[0]
    return pl.pallas_call(
        input_kernel,
        grid=(count,),
        in_specs=[
            image(PATCHES),
            image(HIDDEN),
            image(PATCHES),
            whole((PATCHES, HIDDEN)),
            whole((2, D)),
        ],
        out_specs=[image(PATCHES), whole((1, D))],
        out_shape=[struct((count, PATCHES, D), F32), struct((1, D), F32)],
        compiler_params=params(),
        cost_estimate=pl.CostEstimate(
            flops=2 * count * PATCHES * D * HIDDEN, bytes_accessed=16 * 2**20, transcendentals=0
        ),
        name="input_gradient",
    )(images, da, dx1, w1, gains)


def out_kernel(counts, own_table, other_table, *refs):
    pieces = refs[0:4]
    a0, a1, a2, a3, x1 = refs[4:9]
    out, weights, sems = refs[9:]
    step = pl.program_id(0)

    @pl.when(step == 0)
    def _():
        copies = []
        for at in range(2 * UNITS):
            table = own_table if at < UNITS else other_table
            pair = pieces[0:2] if at < UNITS else pieces[2:4]
            copies += load_unit(table, pair, at % UNITS, weights.at[at], sems.at[at])
        for copy in copies:
            copy.start()
        for copy in copies:
            copy.wait()

    total = dot(a0[...], weights[0], NN)
    total += dot(a1[...], weights[1], NN)
    total += dot(a2[...], weights[2], NN)
    total += dot(a3[...], weights[3], NN)
    for at in range(GROUP):
        keep = (step * GROUP + at < counts[0]).astype(F32)
        out[at] = keep * (x1[at] + total[at * PAD : at * PAD + PATCHES, :])


def block_output(counts, tables, pieces, acts, x1):
    count = x1.shape[0]
    tile = GROUP * PAD
    images = pl.BlockSpec((GROUP, PATCHES, D), lambda i: (i, 0, 0))
    return pl.pallas_call(
        out_kernel,
        grid=(count // GROUP,),
        in_specs=[SMEM, SMEM, SMEM]
        + [ANY] * 4
        + [pl.BlockSpec((tile, F), lambda i: (i, 0))] * 4
        + [images],
        out_specs=images,
        out_shape=struct((count, PATCHES, D), F32),
        scratch_shapes=[
            pltpu.VMEM((2 * UNITS, F, D), BF),
            pltpu.SemaphoreType.DMA((2 * UNITS, BLOCKS)),
        ],
        compiler_params=params(),
        cost_estimate=pl.CostEstimate(
            flops=2 * count * PAD * D * DC, bytes_accessed=24 * 2**20, transcendentals=0
        ),
        name="block_output",
    )(counts, *tables, *pieces, *acts, x1)


class Links:
    def __init__(self, size):
        self.size = size
        self.chips = size // 2
        bits = self.chips.bit_length() - 1
        high = [1 << b for b in range(2, bits)]
        self.orders = (high + [1, 2], high + [2, 1])
        self.index = lax.axis_index("fsdp")
        self.core = self.index & 1
        self.chip = self.index >> 1

    def swap(self, x, mask):
        return lax.ppermute(x, "fsdp", [(i, i ^ mask) for i in range(self.size)])

    def stage(self, x, level):
        pairs = [(i, i ^ (self.orders[i & 1][level] << 1)) for i in range(self.size)]
        return lax.ppermute(x, "fsdp", pairs)

    def owners(self, core):
        place = jnp.arange(self.chips, dtype=jnp.int32)
        owner = jnp.full((self.chips,), self.chip, jnp.int32)
        for level in range(len(self.orders[0])):
            bit = (place >> level) & 1
            mask = jnp.where(core == 0, self.orders[0][level], self.orders[1][level])
            owner = owner ^ (bit * mask)
        return owner

    def places(self, core):
        relative = jnp.arange(self.chips, dtype=jnp.int32) ^ self.chip
        place = jnp.zeros_like(relative)
        for level in range(len(self.orders[0])):
            mask = jnp.where(core == 0, self.orders[0][level], self.orders[1][level])
            place = place | (((relative & mask) != 0).astype(jnp.int32) << level)
        return place

    def table(self, core):
        if self.chips == BLOCKS:
            return jnp.concatenate([self.owners(core), self.places(core)])
        order = jnp.arange(BLOCKS, dtype=jnp.int32)
        return jnp.concatenate([order, order])

    def gather(self, x):
        x = x[None]
        for level in range(len(self.orders[0]) - 1):
            x = jnp.concatenate([x, self.stage(x, level)], axis=0)
        return x, self.stage(x, len(self.orders[0]) - 1)

    def as_blocks(self, halves, core):
        if self.chips == BLOCKS:
            return halves
        x = jnp.take(jnp.concatenate(halves, axis=0), self.places(core), axis=0)
        units = x.shape[1]
        x = x.transpose(1, 0, 2, 3).reshape(units, BLOCKS, TILE, D).transpose(1, 0, 2, 3)
        return x[: BLOCKS // 2], x[BLOCKS // 2 :]

    def from_blocks(self, x, core):
        if self.chips == BLOCKS:
            return x
        return jnp.take(x.reshape(self.chips, -1, D), self.owners(core), axis=0)

    def scatter(self, mine, received):
        x = [(a.astype(F32), b.astype(F32)) for a, b in zip(mine, received)]
        x = jnp.stack([a + b for a, b in x], axis=1)
        for level in reversed(range(len(self.orders[0]))):
            half = x.shape[0] // 2
            x = x[:half] + self.stage(x[half:].astype(BF), level).astype(F32)
        return x[0]

    def gather_flat(self, x):
        mask = 1
        while mask < self.size:
            got = self.swap(x, mask)
            upper = (self.index & mask) != 0
            x = jnp.where(
                upper, jnp.concatenate([got, x], axis=1), jnp.concatenate([x, got], axis=1)
            )
            mask *= 2
        return x

    def scatter_flat(self, x):
        mask = self.size // 2
        while mask:
            half = x.shape[1] // 2
            upper = (self.index & mask) != 0
            keep = jnp.where(upper, x[:, half:], x[:, :half])
            send = jnp.where(upper, x[:, :half], x[:, half:])
            x = keep + self.swap(send.astype(BF), mask).astype(F32)
            mask //= 2
        return x

    def total(self, x):
        mask = 1
        while mask < self.size:
            x = x + self.swap(x, mask)
            mask *= 2
        return x


def shards(
    images,
    cotangent,
    counts,
    w_token_in,
    w_token_out,
    w_chan_in,
    w_chan_out,
    gains,
    row_states,
    col_states,
    gain_states,
):
    links = Links(D * DC // w_chan_in.shape[0])
    size, chips, core = links.size, links.chips, links.core
    count = images.shape[0]
    own_table, other_table = links.table(core), links.table(1 - core)
    tables = (own_table, other_table)

    token = links.gather_flat(jnp.stack([w_token_in, w_token_out]).astype(BF))
    w1 = token[0].reshape(PATCHES, HIDDEN)
    w2 = token[1].reshape(HIDDEN, PATCHES)

    rows3 = D // size
    rows4 = DC // size
    sub = rows4 // UNITS
    local3 = w_chan_in.astype(BF).reshape(rows3, chips, 2, UNITS, sub)
    local3 = local3.transpose(2, 3, 0, 1, 4).reshape(2, UNITS, rows3, F)
    mine = lax.dynamic_index_in_dim(local3, core, 0, keepdims=False)
    theirs = lax.dynamic_index_in_dim(local3, 1 - core, 0, keepdims=False)
    got = links.swap(theirs, 1)
    local3 = jnp.where(
        core == 0, jnp.concatenate([mine, got], axis=1), jnp.concatenate([got, mine], axis=1)
    )
    local4 = w_chan_out.astype(BF).reshape(UNITS, sub, D)
    gathered3 = links.gather(local3)
    gathered4 = links.gather(local4)
    other3 = tuple(links.swap(x, 1) for x in gathered3)
    other4 = tuple(links.swap(x, 1) for x in gathered4)
    own3 = links.as_blocks(gathered3, core)
    own4 = links.as_blocks(gathered4, core)
    other3 = links.as_blocks(other3, 1 - core)
    other4 = links.as_blocks(other4, 1 - core)

    y1, dout = first_norm(counts, images, cotangent, gains)
    h, slope1, x1, y2 = token_forward(images, y1, w1, w2, gains)
    y2_rows = y2.reshape(count * PAD, D)
    dout_rows = dout.reshape(count * PAD, D)
    order = [(own_table, own3, own4, u) for u in range(UNITS)]
    order += [(other_table, other3, other4, u) for u in range(UNITS)]
    acts, slopes, grads4 = [], [], []
    for table, pieces, _, unit in order:
        act, slope, grad = channel_unit(True, unit, table, pieces, y2_rows, dout_rows)
        acts.append(act)
        slopes.append(slope)
        grads4.append(grad)

    def finish(grads):
        grads = [links.from_blocks(g, core if k < UNITS else 1 - core) for k, g in enumerate(grads)]
        received = [links.swap(g, 1) for g in grads[UNITS:]]
        return links.scatter(grads[:UNITS], received)

    dcs, grads3 = [], []
    for (table, _, pieces, unit), slope in zip(order, slopes):
        dc, grad = channel_unit(False, unit, table, pieces, dout_rows, y2_rows, slope)
        dcs.append(dc)
        grads3.append(grad)
    grad4 = finish(grads4).reshape(rows4, D)
    grad3 = finish(grads3)
    mine = lax.dynamic_slice_in_dim(grad3, core * rows3, rows3, 1)
    theirs = lax.dynamic_slice_in_dim(grad3, (1 - core) * rows3, rows3, 1)
    got = links.swap(theirs, 1)
    grad3 = jnp.where(core == 0, jnp.stack([mine, got]), jnp.stack([got, mine]))
    grad3 = grad3.reshape(2, UNITS, rows3, chips, sub).transpose(2, 3, 0, 1, 4).reshape(rows3, DC)

    dx1, da, g1, g2, dg2 = backward(
        tables, own3 + other3, dcs, dout, x1, h, slope1, y1, w2, gains
    )
    token_grads = links.scatter_flat(jnp.stack([g1.reshape(-1), g2.reshape(-1)]))
    token_all = links.gather_flat(token_grads.astype(BF)).astype(F32)
    full = (token_all[0].reshape(PATCHES, HIDDEN), token_all[1].reshape(HIDDEN, PATCHES))
    grad_input, dg1 = input_gradient(images, da, dx1, w1, gains)
    block_out = block_output(counts, tables, own4 + other4, acts, x1)

    edges_r = (0, PATCHES, PATCHES + HIDDEN, PATCHES + HIDDEN + D, PATCHES + HIDDEN + D + DC)
    edges_c = (0, HIDDEN, HIDDEN + PATCHES, HIDDEN + PATCHES + DC, HIDDEN + PATCHES + DC + D)
    old_rows = [row_states[edges_r[k] : edges_r[k + 1]] for k in range(4)]
    old_cols = [col_states[edges_c[k] : edges_c[k + 1]] for k in range(4)]
    masters = (w_token_in, w_token_out, w_chan_in, w_chan_out)
    shapes = ((PATCHES, HIDDEN), (HIDDEN, PATCHES), (D, DC), (DC, D))
    own_rows, parts = [], []
    for which, grad, rows in ((2, grad3, rows3), (3, grad4, rows4)):
        squares = grad * grad + 1e-30
        old = lax.dynamic_slice_in_dim(old_rows[which], links.index * rows, rows)
        row = DECAY * old + (1.0 - DECAY) * jnp.mean(squares, axis=1)
        own_rows.append(row)
        parts.append(
            lax.dynamic_update_slice_in_dim(
                jnp.zeros((shapes[which][0],), F32), row, links.index * rows, 0
            )
        )
        parts.append(jnp.sum(squares, axis=0))
        parts.append(jnp.sum(grad * grad / row[:, None], axis=0))
    parts.append(jnp.stack([jnp.sum(m * m) for m in masters]))
    parts.append(dg1[0])
    parts.append(dg2[0])
    sizes_of = [p.shape[0] for p in parts]
    summed = links.total(jnp.concatenate(parts))
    pieces, at = [], 0
    for length in sizes_of:
        pieces.append(summed[at : at + length])
        at += length
    row3, col3, weighted3, row4, col4, weighted4, weight_squares, dg1, dg2 = pieces

    rows_out, cols_out, update_sizes, new_weights = [None] * 4, [None] * 4, [None] * 4, [None] * 4
    factors = [None] * 4
    for which in range(2):
        row_count, col_count = shapes[which]
        squares = full[which] * full[which]
        row = DECAY * old_rows[which] + (1.0 - DECAY) * jnp.mean(squares + 1e-30, axis=1)
        col = DECAY * old_cols[which] + (1.0 - DECAY) * jnp.mean(squares + 1e-30, axis=0)
        mean_row = jnp.mean(row)
        scaled = squares / (row[:, None] * col[None, :])
        update_sizes[which] = jnp.sqrt(jnp.mean(scaled) * mean_row)
        rows_out[which], cols_out[which] = row, col
        flat = lax.rsqrt(row[:, None] * col[None, :] / mean_row).reshape(-1)
        length = masters[which].shape[0]
        factors[which] = lax.dynamic_slice_in_dim(flat, links.index * length, length)
    for which, row, col_sum, weighted, mine in (
        (2, row3, col3, weighted3, own_rows[0]),
        (3, row4, col4, weighted4, own_rows[1]),
    ):
        row_count, col_count = shapes[which]
        col = DECAY * old_cols[which] + (1.0 - DECAY) * (col_sum / row_count)
        mean_row = jnp.mean(row)
        update_sizes[which] = jnp.sqrt(
            jnp.sum(weighted / col) * mean_row / (row_count * col_count)
        )
        rows_out[which], cols_out[which] = row, col
        factors[which] = lax.rsqrt(mine[:, None] * col[None, :] / mean_row)
    token_grads = [token_grads[0], token_grads[1]]
    own_grads = token_grads + [grad3, grad4]
    for which in range(4):
        row_count, col_count = shapes[which]
        scale = jnp.sqrt(weight_squares[which] / (row_count * col_count) + 1e-06)
        scale = STEP * scale / jnp.maximum(1.0, update_sizes[which] / CLIP)
        update = (own_grads[which] * factors[which] * scale).reshape(-1)
        new_weights[which] = masters[which] - update

    gain_grads = jnp.stack([dg1, dg2])
    gain_stats = DECAY * gain_states + (1.0 - DECAY) * (gain_grads * gain_grads + 1e-30)
    gain_update = gain_grads * lax.rsqrt(gain_stats)
    gain_sizes = jnp.sqrt(jnp.mean(gain_update * gain_update, axis=1))
    gain_update = gain_update / jnp.maximum(1.0, gain_sizes / CLIP)[:, None]
    gain_scale = jnp.sqrt(jnp.mean(gains * gains, axis=1) + 1e-06)
    new_gains = gains - STEP * gain_scale[:, None] * gain_update
    update_rms = jnp.concatenate([jnp.stack(update_sizes), gain_sizes])
    return (
        block_out,
        grad_input,
        token_grads[0],
        token_grads[1],
        grad3.reshape(-1),
        grad4.reshape(-1),
        new_weights[0],
        new_weights[1],
        new_weights[2],
        new_weights[3],
        gain_grads,
        gain_stats,
        new_gains,
        jnp.concatenate(rows_out),
        jnp.concatenate(cols_out),
        update_rms,
    )


def solution(mesh):
    split = P("fsdp")
    images = P("fsdp", None, None)
    in_specs = (images, images) + (split,) * 5 + (P(),) * 4
    out_specs = (images, images) + (split,) * 8 + (P(),) * 6
    return jax.shard_map(
        shards, mesh=mesh, in_specs=in_specs, out_specs=out_specs, check_vma=False
    )
```

time: 848 us -> 423 us (0.50)
  waiting for transfers between devices: 486 us -> 103 us
  Pallas kernels: 0 us -> 166 us
  matrix products: 153 us -> 0 us
  blocking collectives: 79.9 us -> 0 us
  starting transfers between devices: 0.16 us -> 38.4 us
  other arithmetic: 32.9 us -> 50.8 us
  local copies, waits for them, and re-layouts: 65.3 us -> 47.9 us
  between operations: 24.2 us -> 12.3 us
    unnamed x6 -> x0, waiting for transfers between devices: 392 us -> none
    pallas_call x0 -> x13, Pallas kernels: none -> 166 us  [the longest x8 89.7 us: channel_unit(): pl.pallas_call(functools.partial(channel_kernel, unit, forward), grid=(ro...]
    dot_general x24 -> x0, matrix products: 153 us -> none  [the longest x2 25.6 us: shards(): jnp.einsum('bsd,fd->bsf', grad_low, back_four, preferred_element_type=jnp...]
    ppermute x0 -> x46, waiting for transfers between devices: none -> 103 us  [the longest x16 68.9 us: stage(): return lax.ppermute(x, 'fsdp', pairs)]
    all_gather x2 -> x0, waiting for transfers between devices: 94.4 us -> none  [the longest x1 55.7 us: shards(): lax.all_gather(low_copies[2], 'fsdp', axis=0, tiled=True)]
    psum x2 -> x0, blocking collectives: 79.9 us -> none  [the longest x1 40.4 us: shards(): lax.psum((partials[0], partials[1], partials[2], partials[3], partials[4]...]
    ppermute x0 -> x46, starting transfers between devices: none -> 38.4 us  [the longest x16 23.7 us: stage(): return lax.ppermute(x, 'fsdp', pairs)]
    reshape x11 -> x2, local copies, waits for them, and re-layouts: 32.7 us -> 0.69 us  [the longest x1 0.35 us: shards(): local3 = local3.transpose(2, 3, 0, 1, 4).reshape(2, UNITS, rows3, F)]
  transfers between devices with their start and end apart: 4 -> 46, of which waited for: 4 -> 22; matrix products, arithmetic and copies ran while one was open for 10% -> 17% of each run, Pallas kernels for 0% -> 28%
where the time goes in v1:
time: 423 us; the launch traced here: 418 us
  Pallas kernels  166 us (39%)
  waiting for transfers between devices  103 us (24%)
  other arithmetic  50.8 us (12%)
  local copies, waits for them, and re-layouts  47.9 us (11%)
  starting transfers between devices  38.4 us (9%)
  between operations  12.3 us (3%)
    pallas_call x8, Pallas kernels, channel_unit(): pl.pallas_call(functools.partial(channel_kernel, unit, forward), grid=(ro...  89.7 us
    ppermute x16, waiting for transfers between devices, stage(): return lax.ppermute(x, 'fsdp', pairs)  68.9 us
    ppermute x30, waiting for transfers between devices, swap(): return lax.ppermute(x, 'fsdp', [(i, i ^ mask) for i in range(self.size)])  33.9 us
    pallas_call x1, Pallas kernels, backward(): pl.pallas_call(back_kernel, grid=(count // GROUP,), in_specs=[SMEM, SMEM]...  28.8 us
    unnamed x112, local copies, waits for them, and re-layouts  25 us
    ppermute x16, starting transfers between devices, stage(): return lax.ppermute(x, 'fsdp', pairs)  23.7 us
    pallas_call x1, Pallas kernels, block_output(): pl.pallas_call(out_kernel, grid=(count // GROUP,), in_specs=[SMEM, SMEM,...  15.5 us
    ppermute x30, starting transfers between devices, swap(): return lax.ppermute(x, 'fsdp', [(i, i ^ mask) for i in range(self.size)])  14.7 us
  transfers between devices with their start and end apart: 46, of which 22 were waited for; matrix products, arithmetic and copies ran while one was open for 17% of the time, Pallas kernels for 28%

profile of v1, /device:TPU:0, one launch (start us, length us, event | category | flops | bytes accessed | tf_op | source)
XLA Modules:
  0.0 417.9 jit_solution(8174731602462355162)
XLA Ops:
  0.7 1.5 multiply_reduce_fusion.3
  2.2 1.4 multiply_reduce_fusion.2
  4.1 1.7 multiply_reduce_fusion.1
  7.6 3.1 collective-permute-start
  12.6 1.9 copy.59.x
  15.1 1.9 copy.58.cot
  17.0 8.2 %first_norm.1 = (bf16[8,196,768]{2,1,0:T(8,128)(2,1)}, bf16[8,208,768]{2,1,0:T(8,128)(2,1)}) custom-call(s32[1]{0:T(128)S(6)} %copy.74.counts, bf16[8,196,768]{2,1,0:T(8,128)(2,1)} %copy.59.x, bf16[8,196,768]{2,1,0:T(8,128)(2,1)} %copy.58.cot, f32[2,768]{1,0:T(2,128)} %gains.5), custom_call_target="tpu_custom_call" | custom-call | tf_op jit(solution)/shard_map/first_norm/pallas_call | solution.py:91
  25.4 1.6 collective-permute-start.12
  27.5 1.7 collective-permute-done.12
  29.3 1.6 collective-permute-start.13
  30.9 2.7 collective-permute-start.1
  33.6 2.9 collective-permute-start.8
  36.8 16.3 %collective-permute-done.1 = bf16[2,2,48,768]{3,2,1,0:T(8,128)(2,1)S(1)} collective-permute-done((bf16[2,2,48,768]{3,2,1,0:T(8,128)(2,1)S(1)}, bf16[2,2,48,768]{3,2,1,0:T(8,128)(2,1)S(1)}, u32[]{:S(2)}, u32[]{:S(2)}) %collective-permute-start.1) | collective-permute-done | bytes 294944 | tf_op jit(solution)/shard_map/ppermute | solution.py:414
  54.0 4.0 collective-permute-done.8
  58.1 1.6 collective-permute-start.9
  61.4 1.7 collective-permute-done.2
  65.0 10.1 %collective-permute-done.9 = bf16[4,2,48,768]{3,2,1,0:T(8,128)(2,1)S(1)} collective-permute-done((bf16[4,2,48,768]{3,2,1,0:T(8,128)(2,1)S(1)}, bf16[4,2,48,768]{3,2,1,0:T(8,128)(2,1)S(1)}, u32[]{:S(2)}, u32[]{:S(2)}) %collective-permute-start.9) | collective-permute-done | bytes 589856 | tf_op jit(solution)/shard_map/ppermute | solution.py:414
  75.3 1.3 collective-permute-start.10
  77.1 1.6 slice_reduce_fusion
  80.7 13.0 %token_forward.1 = (bf16[8,384,768]{2,1,0:T(8,128)(2,1)}, bf16[8,384,768]{2,1,0:T(8,128)(2,1)}, f32[8,196,768]{2,1,0:T(8,128)}, bf16[8,208,768]{2,1,0:T(8,128)(2,1)}) custom-call(bf16[8,196,768]{2,1,0:T(8,128)(2,1)} %copy.59.x, bf16[8,196,768]{2,1,0:T(8,128)(2,1)} %get-tuple-element.49.y1.refs_12_, bf16[196,384]{1,0:T(8,128)(2,1)} %reshape_squeeze.4.w1, ...), custom_call_target="tpu_custom_call" | custom-call | tf_op jit(solution)/shard_map/token_forward/pallas_call | solution.py:116
  95.3 12.2 %channel_forward.5 = (bf16[1664,768]{1,0:T(8,128)(2,1)}, bf16[1664,768]{1,0:T(8,128)(2,1)}, bf16[16,48,768]{2,1,0:T(8,128)(2,1)}) custom-call(s32[32]{0:T(128)} %pad_add_fusion.table.own_table, bf16[8,2,48,768]{3,2,1,0:T(8,128)(2,1)} %copy-done.7, bf16[8,2,48,768]{3,2,1,0:T(8,128)(2,1)} %copy-done.13, bf16[1664,768]{1,0:T(8,128)(2,1)} %bitcast.66, ...), custom_call_target="tpu_custom_call" | custom-call | flops 3925868544 | bytes 12582912 | tf_op jit(solution)/shard_map/channel_forward/pallas_call | solution.py:203
  107.5 11.4 %channel_forward.4 = (bf16[1664,768]{1,0:T(8,128)(2,1)}, bf16[1664,768]{1,0:T(8,128)(2,1)}, bf16[16,48,768]{2,1,0:T(8,128)(2,1)}) custom-call(s32[32]{0:T(128)} %pad_add_fusion.table.own_table, bf16[8,2,48,768]{3,2,1,0:T(8,128)(2,1)} %copy-done.7, bf16[8,2,48,768]{3,2,1,0:T(8,128)(2,1)} %copy-done.13, bf16[1664,768]{1,0:T(8,128)(2,1)} %bitcast.67, ...), custom_call_target="tpu_custom_call" | custom-call | flops 3925868544 | bytes 12582912 | tf_op jit(solution)/shard_map/channel_forward/pallas_call | solution.py:203
  118.9 11.1 %channel_backward.5 = (bf16[1664,768]{1,0:T(8,128)(2,1)}, bf16[16,48,768]{2,1,0:T(8,128)(2,1)}) custom-call(s32[32]{0:T(128)} %pad_add_fusion.table.own_table, bf16[8,2,48,768]{3,2,1,0:T(8,128)(2,1)} %constant_dynamic-update-slice_fusion.refs_0_.lo, bf16[8,2,48,768]{3,2,1,0:T(8,128)(2,1)} %collective-permute-done.3.refs_1_.hi, bf16[1664,768]{1,0:T(8,128)(2,1)} %bitcast.55, ...), custom_call_target="tpu_custom_call" | custom-call | flops 3925868544 | bytes 12582912 | tf_op jit(solution)/shard_map/channel_backward/pallas_call | solution.py:203
  130.0 10.2 %channel_backward.4 = (bf16[1664,768]{1,0:T(8,128)(2,1)}, bf16[16,48,768]{2,1,0:T(8,128)(2,1)}) custom-call(s32[32]{0:T(128)} %pad_add_fusion.table.own_table, bf16[8,2,48,768]{3,2,1,0:T(8,128)(2,1)} %constant_dynamic-update-slice_fusion.refs_0_.lo, bf16[8,2,48,768]{3,2,1,0:T(8,128)(2,1)} %collective-permute-done.3.refs_1_.hi, bf16[1664,768]{1,0:T(8,128)(2,1)} %bitcast.56, ...), custom_call_target="tpu_custom_call" | custom-call | flops 3925868544 | bytes 12582912 | tf_op jit(solution)/shard_map/channel_backward/pallas_call | solution.py:203
  142.2 12.1 %channel_forward.7 = (bf16[1664,768]{1,0:T(8,128)(2,1)}, bf16[1664,768]{1,0:T(8,128)(2,1)}, bf16[16,48,768]{2,1,0:T(8,128)(2,1)}) custom-call(s32[32]{0:T(128)} %pad_add_fusion.1.table.other_table, bf16[8,2,48,768]{3,2,1,0:T(8,128)(2,1)} %copy-done.14, bf16[8,2,48,768]{3,2,1,0:T(8,128)(2,1)} %copy-done.15, bf16[1664,768]{1,0:T(8,128)(2,1)} %bitcast.70, ...), custom_call_target="tpu_custom_call" | custom-call | flops 3925868544 | bytes 12582912 | tf_op jit(solution)/shard_map/channel_forward/pallas_call | solution.py:203
  154.3 11.3 %channel_forward.6 = (bf16[1664,768]{1,0:T(8,128)(2,1)}, bf16[1664,768]{1,0:T(8,128)(2,1)}, bf16[16,48,768]{2,1,0:T(8,128)(2,1)}) custom-call(s32[32]{0:T(128)} %pad_add_fusion.1.table.other_table, bf16[8,2,48,768]{3,2,1,0:T(8,128)(2,1)} %copy-done.14, bf16[8,2,48,768]{3,2,1,0:T(8,128)(2,1)} %copy-done.15, bf16[1664,768]{1,0:T(8,128)(2,1)} %bitcast.71, ...), custom_call_target="tpu_custom_call" | custom-call | flops 3925868544 | bytes 12582912 | tf_op jit(solution)/shard_map/channel_forward/pallas_call | solution.py:203
  167.1 11.3 %channel_backward.7 = (bf16[1664,768]{1,0:T(8,128)(2,1)}, bf16[16,48,768]{2,1,0:T(8,128)(2,1)}) custom-call(s32[32]{0:T(128)} %pad_add_fusion.1.table.other_table, bf16[8,2,48,768]{3,2,1,0:T(8,128)(2,1)} %copy-done.49, bf16[8,2,48,768]{3,2,1,0:T(8,128)(2,1)} %copy-done.50, bf16[1664,768]{1,0:T(8,128)(2,1)} %bitcast.59, bf16[1664,768]{1,0:T(8,128)(2,1)} %bitcast.72, ...), custom_call_target="tpu_custom_call" | custom-call | flops 3925868544 | bytes 12582912 | tf_op jit(solution)/shard_map/channel_backward/pallas_call | solution.py:203
  178.4 10.1 %channel_backward.6 = (bf16[1664,768]{1,0:T(8,128)(2,1)}, bf16[16,48,768]{2,1,0:T(8,128)(2,1)}) custom-call(s32[32]{0:T(128)} %pad_add_fusion.1.table.other_table, bf16[8,2,48,768]{3,2,1,0:T(8,128)(2,1)} %copy-done.49, bf16[8,2,48,768]{3,2,1,0:T(8,128)(2,1)} %copy-done.50, bf16[1664,768]{1,0:T(8,128)(2,1)} %bitcast.60, bf16[1664,768]{1,0:T(8,128)(2,1)} %bitcast.73, ...), custom_call_target="tpu_custom_call" | custom-call | flops 3925868544 | bytes 12582912 | tf_op jit(solution)/shard_map/channel_backward/pallas_call | solution.py:203
  188.5 28.8 %backward.1 = (f32[8,196,768]{2,1,0:T(8,128)}, bf16[8,384,768]{2,1,0:T(8,128)(2,1)}, f32[196,384]{1,0:T(8,128)}, f32[384,196]{1,0:T(8,128)}, f32[1,768]{1,0:T(1,128)}) custom-call(s32[32]{0:T(128)} %pad_add_fusion.table.own_table, s32[32]{0:T(128)} %pad_add_fusion.1.table.other_table, bf16[8,2,48,768]{3,2,1,0:T(8,128)(2,1)} %copy-done.7, ...), custom_call_target="tpu_custom_call" | custom-call | flops 7851737088 | bytes 41943040 | tf_op jit(solution)/shard_map/backward/pallas_call | solution.py:272
  217.3 1.4 copy.66
  218.7 1.6 stack_reshape.7
  220.9 9.9 %collective-permute-done.18 = bf16[2,37632]{1,0:T(2,128)(2,1)S(1)} collective-permute-done((bf16[2,37632]{1,0:T(2,128)(2,1)S(1)}, bf16[2,37632]{1,0:T(2,128)(2,1)S(1)}, u32[]{:S(2)}, u32[]{:S(2)}) %collective-permute-start.18) | collective-permute-done | bytes 150560 | tf_op jit(solution)/shard_map/ppermute | solution.py:410
  231.5 4.4 %collective-permute-done.19 = bf16[2,18816]{1,0:T(2,128)(2,1)S(1)} collective-permute-done((bf16[2,18816]{1,0:T(2,128)(2,1)S(1)}, bf16[2,18816]{1,0:T(2,128)(2,1)S(1)}, u32[]{:S(2)}, u32[]{:S(2)}) %collective-permute-start.19) | collective-permute-done | bytes 75296 | tf_op jit(solution)/shard_map/ppermute | solution.py:410
  237.1 3.0 collective-permute-done.20
  241.6 2.6 collective-permute-done.21
  250.2 15.5 %block_output.1 = f32[8,196,768]{2,1,0:T(8,128)} custom-call(s32[1]{0:T(128)S(6)} %copy.74.counts, s32[32]{0:T(128)} %pad_add_fusion.table.own_table, s32[32]{0:T(128)} %pad_add_fusion.1.table.other_table, bf16[8,2,48,768]{3,2,1,0:T(8,128)(2,1)} %constant_dynamic-update-slice_fusion.refs_0_.lo, bf16[8,2,48,768]{3,2,1,0:T(8,128)(2,1)} %collective-permute-done.3.refs_1_.hi, ...), custom_call_target="tpu_custom_call" | custom-call | flops 7851737088 | bytes 25165824 | tf_op jit(solution)/shard_map/block_output/pallas_call | solution.py:377
  267.1 10.5 %input_gradient.1 = (f32[8,196,768]{2,1,0:T(8,128)}, f32[1,768]{1,0:T(1,128)}) custom-call(bf16[8,196,768]{2,1,0:T(8,128)(2,1)} %copy.59.x, bf16[8,384,768]{2,1,0:T(8,128)(2,1)} %get-tuple-element.67.da, f32[8,196,768]{2,1,0:T(8,128)} %get-tuple-element.68.dx1, bf16[196,384]{1,0:T(8,128)(2,1)} %reshape_squeeze.4.w1, f32[2,768]{1,0:T(2,128)} %gains.5), custom_call_target="tpu_custom_call" | custom-call | flops 924844032 | bytes 16777216 | tf_op jit(solution)/shard_map/input_gradient/pallas_call | solution.py:326
  279.5 6.3 %copy.65 = f32[8,196,768]{2,0,1:T(8,128)} copy(f32[8,196,768]{2,1,0:T(8,128)} %get-tuple-element.147) | data formatting | bytes 9633792
  285.8 3.7 copy.64
  290.6 3.5 collective-permute-done.39
  295.5 1.7 add_bitcast_fusion
  297.2 1.6 add_bitcast_fusion.1
  301.5 1.7 add_bitcast_fusion.2
  303.2 2.4 add_bitcast_fusion.3
  305.6 1.4 fusion.5
  309.0 2.6 add_reduce_fusion.2
  311.6 1.5 add.236
  313.7 3.3 collective-permute-done.32
  317.1 2.0 fusion.1
  320.3 15.8 %collective-permute-done.25 = bf16[8,2,48,768]{3,2,0,1:T(8,128)(2,1)} collective-permute-done((bf16[8,2,48,768]{3,2,0,1:T(8,128)(2,1)}, bf16[8,2,48,768]{3,2,0,1:T(8,128)(2,1)}, u32[]{:S(2)}, u32[]{:S(2)}) %collective-permute-start.25) | collective-permute-done | bytes 1179680 | tf_op jit(solution)/shard_map/ppermute | solution.py:414
  336.0 1.5 fusion.3
  339.4 1.4 fusion.29
  342.2 1.5 slice_add_fusion
  344.5 2.6 collective-permute-start.34
  347.1 1.5 collective-permute-done.26
  350.9 3.0 collective-permute-start.27
  354.0 1.7 add.217
  355.7 9.5 %collective-permute-done.34 = bf16[2,2,48,768]{3,2,0,1:T(8,128)(2,1)} collective-permute-done((bf16[2,2,48,768]{3,2,0,1:T(8,128)(2,1)}, bf16[2,2,48,768]{3,2,0,1:T(8,128)(2,1)}, u32[]{:S(2)}, u32[]{:S(2)}) %collective-permute-start.34) | collective-permute-done | bytes 294944 | tf_op jit(solution)/shard_map/ppermute | solution.py:414
  366.5 2.6 collective-permute-done.27
  370.3 3.0 collective-permute-done.35
  379.0 2.7 concatenate.155
  384.6 2.6 collective-permute-done.42
  392.5 3.0 collective-permute-done.44
  396.5 1.8 divide_reduce_fusion.1
  (286 shorter events, 72.6 us)
Async XLA Ops:
  3.6 21.7 %collective-permute-start.11 = (bf16[2,2352]{1,0:T(2,128)(2,1)S(1)}, bf16[2,2352]{1,0:T(2,128)(2,1)S(1)}, u32[]{:S(2)}, u32[]{:S(2)}) collective-permute-start(bf16[2,2352]{1,0:T(2,128)(2,1)S(1)} %pad_maximum_fusion.8), channel_id=1, source_target_pairs={{0,1},{1,0},{2,3},{3,2},{4,5},{5,4},{6,7},{7,6},{8,9},{9,8},{10,11... | collective-permute-start | bytes 28232 | tf_op jit(solution)/shard_map/ppermute | solution.py:410
  6.6 20.3 %collective-permute-start.6 = (bf16[2,24,768]{2,1,0:T(8,128)(2,1)S(1)}, bf16[2,24,768]{2,1,0:T(8,128)(2,1)S(1)}, u32[]{:S(2)}, u32[]{:S(2)}) collective-permute-start(bf16[2,24,768]{2,1,0:T(8,128)(2,1)S(1)} %get-tuple-element.208), channel_id=1, source_target_pairs={{0,1},{1,0},{2,3},{3,2},{4,5},{5,4},{6,7},{7,6},{8,9},{9,8},{10,11... | collective-permute-start | bytes 221192 | tf_op jit(solution)/shard_map/ppermute | solution.py:410
  7.6 23.3 %collective-permute-start = (bf16[1,2,48,768]{3,2,1,0:T(8,128)(2,1)S(1)}, bf16[1,2,48,768]{3,2,1,0:T(8,128)(2,1)S(1)}, u32[]{:S(2)}, u32[]{:S(2)}) collective-permute-start(bf16[1,2,48,768]{3,2,1,0:T(8,128)(2,1)S(1)} %broadcast_in_dim_reshape.3), channel_id=1, source_target_pairs={{0,8},{1,9},{2,10},{3,11},{4,12},{5,13},{6,14},{7,15},{8,0},{9,1},... | collective-permute-start | bytes 442376 | tf_op jit(solution)/shard_map/ppermute | solution.py:414
  25.4 3.8 collective-permute-start.12
  27.0 6.6 %collective-permute-start.7 = (bf16[1,2,48,768]{3,2,1,0:T(8,128)(2,1)S(1)}, bf16[1,2,48,768]{3,2,1,0:T(8,128)(2,1)S(1)}, u32[]{:S(2)}, u32[]{:S(2)}) collective-permute-start(bf16[1,2,48,768]{3,2,1,0:T(8,128)(2,1)S(1)} %maximum_select_fusion.1), channel_id=1, source_target_pairs={{0,8},{1,9},{2,10},{3,11},{4,12},{5,13},{6,14},{7,15},{8,0},{9,1},... | collective-permute-start | bytes 442376 | tf_op jit(solution)/shard_map/ppermute | solution.py:414
  29.3 7.2 %collective-permute-start.13 = (bf16[2,9408]{1,0:T(2,128)(2,1)S(1)}, bf16[2,9408]{1,0:T(2,128)(2,1)S(1)}, u32[]{:S(2)}, u32[]{:S(2)}) collective-permute-start(bf16[2,9408]{1,0:T(2,128)(2,1)S(1)} %broadcast_select_fusion.7), channel_id=1, source_target_pairs={{0,4},{1,5},{2,6},{3,7},{4,0},{5,1},{6,2},{7,3},{8,12},{9,13},{10,... | collective-permute-start | bytes 112904 | tf_op jit(solution)/shard_map/ppermute | solution.py:410
  30.9 22.2 %collective-permute-start.1 = (bf16[2,2,48,768]{3,2,1,0:T(8,128)(2,1)S(1)}, bf16[2,2,48,768]{3,2,1,0:T(8,128)(2,1)S(1)}, u32[]{:S(2)}, u32[]{:S(2)}) collective-permute-start(bf16[2,2,48,768]{3,2,1,0:T(8,128)(2,1)S(1)} %pad_maximum_fusion.6), channel_id=1, source_target_pairs={{0,16},{1,17},{2,18},{3,19},{4,20},{5,21},{6,22},{7,23},{8,24},{9,... | collective-permute-start | bytes 884744 | tf_op jit(solution)/shard_map/ppermute | solution.py:414
  33.6 24.4 %collective-permute-start.8 = (bf16[2,2,48,768]{3,2,1,0:T(8,128)(2,1)S(1)}, bf16[2,2,48,768]{3,2,1,0:T(8,128)(2,1)S(1)}, u32[]{:S(2)}, u32[]{:S(2)}) collective-permute-start(bf16[2,2,48,768]{3,2,1,0:T(8,128)(2,1)S(1)} %pad_maximum_fusion.7), channel_id=1, source_target_pairs={{0,16},{1,17},{2,18},{3,19},{4,20},{5,21},{6,22},{7,23},{8,24},{9,... | collective-permute-start | bytes 884744 | tf_op jit(solution)/shard_map/ppermute | solution.py:414
  36.7 23.0 %collective-permute-start.14 = (bf16[2,18816]{1,0:T(2,128)(2,1)S(1)}, bf16[2,18816]{1,0:T(2,128)(2,1)S(1)}, u32[]{:S(2)}, u32[]{:S(2)}) collective-permute-start(bf16[2,18816]{1,0:T(2,128)(2,1)S(1)} %broadcast_select_fusion.5), channel_id=1, source_target_pairs={{0,8},{1,9},{2,10},{3,11},{4,12},{5,13},{6,14},{7,15},{8,0},{9,1},... | collective-permute-start | bytes 225800 | tf_op jit(solution)/shard_map/ppermute | solution.py:410
  53.2 9.9 %collective-permute-start.2 = (bf16[4,2,48,768]{3,2,1,0:T(8,128)(2,1)S(1)}, bf16[4,2,48,768]{3,2,1,0:T(8,128)(2,1)S(1)}, u32[]{:S(2)}, u32[]{:S(2)}) collective-permute-start(bf16[4,2,48,768]{3,2,1,0:T(8,128)(2,1)S(1)} %pad_maximum_fusion.3), channel_id=1, source_target_pairs={{0,2},{1,5},{2,0},{3,7},{4,6},{5,1},{6,4},{7,3},{8,10},{9,13},{10,... | collective-permute-start | bytes 1769480 | tf_op jit(solution)/shard_map/ppermute | solution.py:414
  58.1 17.0 %collective-permute-start.9 = (bf16[4,2,48,768]{3,2,1,0:T(8,128)(2,1)S(1)}, bf16[4,2,48,768]{3,2,1,0:T(8,128)(2,1)S(1)}, u32[]{:S(2)}, u32[]{:S(2)}) collective-permute-start(bf16[4,2,48,768]{3,2,1,0:T(8,128)(2,1)S(1)} %pad_maximum_fusion.4), channel_id=1, source_target_pairs={{0,2},{1,5},{2,0},{3,7},{4,6},{5,1},{6,4},{7,3},{8,10},{9,13},{10,... | collective-permute-start | bytes 1769480 | tf_op jit(solution)/shard_map/ppermute | solution.py:414
  59.9 16.7 %collective-permute-start.15 = (bf16[2,37632]{1,0:T(2,128)(2,1)S(1)}, bf16[2,37632]{1,0:T(2,128)(2,1)S(1)}, u32[]{:S(2)}, u32[]{:S(2)}) collective-permute-start(bf16[2,37632]{1,0:T(2,128)(2,1)S(1)} %broadcast_select_fusion.3), channel_id=1, source_target_pairs={{0,16},{1,17},{2,18},{3,19},{4,20},{5,21},{6,22},{7,23},{8,24},{9,... | collective-permute-start | bytes 451592 | tf_op jit(solution)/shard_map/ppermute | solution.py:410
  64.0 30.2 %collective-permute-start.3 = (bf16[8,2,48,768]{3,2,1,0:T(8,128)(2,1)}, bf16[8,2,48,768]{3,2,1,0:T(8,128)(2,1)}, u32[]{:S(2)}, u32[]{:S(2)}) collective-permute-start(bf16[8,2,48,768]{3,2,1,0:T(8,128)(2,1)} %constant_dynamic-update-slice_fusion.refs_0_.lo), channel_id=1, source_target_pairs={{0,4},{1,3},{2,6},{3,1},{4,0},{5,7},{6,2},{7,5},{8,12},{9,11},{10,... | collective-permute-start | bytes 3538952 | tf_op jit(solution)/shard_map/ppermute | solution.py:414
  75.2 18.5 %copy-start.7 = (bf16[8,2,48,768]{3,2,1,0:T(8,128)(2,1)}, bf16[8,2,48,768]{3,2,1,0:T(8,128)(2,1)S(1)}, u32[]{:S(2)}) copy-start(bf16[8,2,48,768]{3,2,1,0:T(8,128)(2,1)S(1)} %pad_maximum_fusion.2.lo.refs_0_) | copy-start | bytes 3538948
  75.3 19.0 %collective-permute-start.10 = (bf16[8,2,48,768]{3,2,1,0:T(8,128)(2,1)S(1)}, bf16[8,2,48,768]{3,2,1,0:T(8,128)(2,1)S(1)}, u32[]{:S(2)}, u32[]{:S(2)}) collective-permute-start(bf16[8,2,48,768]{3,2,1,0:T(8,128)(2,1)S(1)} %pad_maximum_fusion.2.lo.refs_0_), channel_id=1, source_target_pairs={{0,4},{1,3},{2,6},{3,1},{4,0},{5,7},{6,2},{7,5},{8,12},{9,11},{10,... | collective-permute-start | bytes 3538952 | tf_op jit(solution)/shard_map/ppermute | solution.py:414
  93.7 72.0 %collective-permute-start.4 = (bf16[8,2,48,768]{3,2,1,0:T(8,128)(2,1)}, bf16[8,2,48,768]{3,2,1,0:T(8,128)(2,1)S(1)}, u32[]{:S(2)}, u32[]{:S(2)}) collective-permute-start(bf16[8,2,48,768]{3,2,1,0:T(8,128)(2,1)} %constant_dynamic-update-slice_fusion.refs_0_.lo), channel_id=1, source_target_pairs={{0,1},{1,0},{2,3},{3,2},{4,5},{5,4},{6,7},{7,6},{8,9},{9,8},{10,11... | collective-permute-start | bytes 3538952 | tf_op jit(solution)/shard_map/ppermute | solution.py:410
  93.7 46.5 %collective-permute-start.16 = (bf16[8,2,48,768]{3,2,1,0:T(8,128)(2,1)S(1)}, bf16[8,2,48,768]{3,2,1,0:T(8,128)(2,1)S(1)}, u32[]{:S(2)}, u32[]{:S(2)}) collective-permute-start(bf16[8,2,48,768]{3,2,1,0:T(8,128)(2,1)S(1)} %pad_maximum_fusion.2.lo.refs_0_), channel_id=1, source_target_pairs={{0,1},{1,0},{2,3},{3,2},{4,5},{5,4},{6,7},{7,6},{8,9},{9,8},{10,11... | collective-permute-start | bytes 3538952 | tf_op jit(solution)/shard_map/ppermute | solution.py:410
  94.2 71.5 %collective-permute-start.5 = (bf16[8,2,48,768]{3,2,1,0:T(8,128)(2,1)}, bf16[8,2,48,768]{3,2,1,0:T(8,128)(2,1)S(1)}, u32[]{:S(2)}, u32[]{:S(2)}) collective-permute-start(bf16[8,2,48,768]{3,2,1,0:T(8,128)(2,1)} %collective-permute-done.3.refs_1_.hi), channel_id=1, source_target_pairs={{0,1},{1,0},{2,3},{3,2},{4,5},{5,4},{6,7},{7,6},{8,9},{9,8},{10,11... | collective-permute-start | bytes 3538952 | tf_op jit(solution)/shard_map/ppermute | solution.py:410
  94.3 45.9 %collective-permute-start.17 = (bf16[8,2,48,768]{3,2,1,0:T(8,128)(2,1)S(1)}, bf16[8,2,48,768]{3,2,1,0:T(8,128)(2,1)S(1)}, u32[]{:S(2)}, u32[]{:S(2)}) collective-permute-start(bf16[8,2,48,768]{3,2,1,0:T(8,128)(2,1)S(1)} %collective-permute-done.10.hi.refs_1_), channel_id=1, source_target_pairs={{0,1},{1,0},{2,3},{3,2},{4,5},{5,4},{6,7},{7,6},{8,9},{9,8},{10,11... | collective-permute-start | bytes 3538952 | tf_op jit(solution)/shard_map/ppermute | solution.py:410
  217.3 27.2 %copy-start.26 = (f32[2,768]{1,0:T(2,128)S(1)}, f32[2,768]{1,0:T(2,128)}, u32[]{:S(2)}) copy-start(f32[2,768]{1,0:T(2,128)} %gains.5) | copy-start | bytes 18436
  217.3 29.2 %copy-start.34 = (f32[4420]{0:T(1024)S(1)}, f32[4420]{0:T(1024)}, u32[]{:S(2)}) copy-start(f32[4420]{0:T(1024)} %param.19) | copy-start | bytes 53044
  217.3 30.5 %copy-start.48 = (bf16[16,48,768]{2,1,0:T(8,128)(2,1)S(1)}, bf16[16,48,768]{2,1,0:T(8,128)(2,1)}, u32[]{:S(2)}) copy-start(bf16[16,48,768]{2,1,0:T(8,128)(2,1)} %get-tuple-element.79) | copy-start | bytes 3538948
  220.8 9.9 %collective-permute-start.18 = (bf16[2,37632]{1,0:T(2,128)(2,1)S(1)}, bf16[2,37632]{1,0:T(2,128)(2,1)S(1)}, u32[]{:S(2)}, u32[]{:S(2)}) collective-permute-start(bf16[2,37632]{1,0:T(2,128)(2,1)S(1)} %select_convert_fusion), channel_id=1, source_target_pairs={{0,16},{1,17},{2,18},{3,19},{4,20},{5,21},{6,22},{7,23},{8,24},{9,... | collective-permute-start | bytes 451592 | tf_op jit(solution)/shard_map/ppermute | solution.py:410
  231.4 4.4 %collective-permute-start.19 = (bf16[2,18816]{1,0:T(2,128)(2,1)S(1)}, bf16[2,18816]{1,0:T(2,128)(2,1)S(1)}, u32[]{:S(2)}, u32[]{:S(2)}) collective-permute-start(bf16[2,18816]{1,0:T(2,128)(2,1)S(1)} %select_convert_fusion.1), channel_id=1, source_target_pairs={{0,8},{1,9},{2,10},{3,11},{4,12},{5,13},{6,14},{7,15},{8,0},{9,1},... | collective-permute-start | bytes 225800 | tf_op jit(solution)/shard_map/ppermute | solution.py:410
  236.1 4.0 collective-permute-start.20
  240.4 3.8 collective-permute-start.21
  244.4 1.2 collective-permute-start.22
  245.7 3.2 collective-permute-start.36
  247.9 46.5 %collective-permute-start.31 = (bf16[16,48,768]{2,1,0:T(8,128)(2,1)S(1)}, bf16[16,48,768]{2,1,0:T(8,128)(2,1)S(1)}, u32[]{:S(2)}, u32[]{:S(2)}) collective-permute-start(bf16[16,48,768]{2,1,0:T(8,128)(2,1)S(1)} %copy-done.48), channel_id=1, source_target_pairs={{0,1},{1,0},{2,3},{3,2},{4,5},{5,4},{6,7},{7,6},{8,9},{9,8},{10,11... | collective-permute-start | bytes 3538952 | tf_op jit(solution)/shard_map/ppermute | solution.py:410
  248.2 48.9 %collective-permute-start.30 = (bf16[16,48,768]{2,1,0:T(8,128)(2,1)}, bf16[16,48,768]{2,1,0:T(8,128)(2,1)}, u32[]{:S(2)}, u32[]{:S(2)}) collective-permute-start(bf16[16,48,768]{2,1,0:T(8,128)(2,1)} %get-tuple-element.77), channel_id=1, source_target_pairs={{0,1},{1,0},{2,3},{3,2},{4,5},{5,4},{6,7},{7,6},{8,9},{9,8},{10,11... | collective-permute-start | bytes 3538952 | tf_op jit(solution)/shard_map/ppermute | solution.py:410
  248.4 53.1 %collective-permute-start.24 = (bf16[16,48,768]{2,1,0:T(8,128)(2,1)}, bf16[16,48,768]{2,1,0:T(8,128)(2,1)}, u32[]{:S(2)}, u32[]{:S(2)}) collective-permute-start(bf16[16,48,768]{2,1,0:T(8,128)(2,1)} %get-tuple-element.75), channel_id=1, source_target_pairs={{0,1},{1,0},{2,3},{3,2},{4,5},{5,4},{6,7},{7,6},{8,9},{9,8},{10,11... | collective-permute-start | bytes 3538952 | tf_op jit(solution)/shard_map/ppermute | solution.py:410
  248.7 54.4 %collective-permute-start.23 = (bf16[16,48,768]{2,1,0:T(8,128)(2,1)}, bf16[16,48,768]{2,1,0:T(8,128)(2,1)}, u32[]{:S(2)}, u32[]{:S(2)}) collective-permute-start(bf16[16,48,768]{2,1,0:T(8,128)(2,1)} %get-tuple-element.73), channel_id=1, source_target_pairs={{0,1},{1,0},{2,3},{3,2},{4,5},{5,4},{6,7},{7,6},{8,9},{9,8},{10,11... | collective-permute-start | bytes 3538952 | tf_op jit(solution)/shard_map/ppermute | solution.py:410
  249.0 16.8 %collective-permute-start.37 = (bf16[2,4704]{1,0:T(2,128)(2,1)S(1)}, bf16[2,4704]{1,0:T(2,128)(2,1)S(1)}, u32[]{:S(2)}, u32[]{:S(2)}) collective-permute-start(bf16[2,4704]{1,0:T(2,128)(2,1)S(1)} %broadcast_select_fusion.8), channel_id=1, source_target_pairs={{0,2},{1,3},{2,0},{3,1},{4,6},{5,7},{6,4},{7,5},{8,10},{9,11},{10,... | collective-permute-start | bytes 56456 | tf_op jit(solution)/shard_map/ppermute | solution.py:410
  265.9 23.6 %collective-permute-start.38 = (bf16[2,9408]{1,0:T(2,128)(2,1)S(1)}, bf16[2,9408]{1,0:T(2,128)(2,1)S(1)}, u32[]{:S(2)}, u32[]{:S(2)}) collective-permute-start(bf16[2,9408]{1,0:T(2,128)(2,1)S(1)} %broadcast_select_fusion.6), channel_id=1, source_target_pairs={{0,4},{1,5},{2,6},{3,7},{4,0},{5,1},{6,2},{7,3},{8,12},{9,13},{10,... | collective-permute-start | bytes 112904 | tf_op jit(solution)/shard_map/ppermute | solution.py:410
  289.6 4.4 %collective-permute-start.39 = (bf16[2,18816]{1,0:T(2,128)(2,1)S(1)}, bf16[2,18816]{1,0:T(2,128)(2,1)S(1)}, u32[]{:S(2)}, u32[]{:S(2)}) collective-permute-start(bf16[2,18816]{1,0:T(2,128)(2,1)S(1)} %broadcast_select_fusion.4), channel_id=1, source_target_pairs={{0,8},{1,9},{2,10},{3,11},{4,12},{5,13},{6,14},{7,15},{8,0},{9,1},... | collective-permute-start | bytes 225800 | tf_op jit(solution)/shard_map/ppermute | solution.py:410
  294.3 14.3 %collective-permute-start.40 = (bf16[2,37632]{1,0:T(2,128)(2,1)S(1)}, bf16[2,37632]{1,0:T(2,128)(2,1)S(1)}, u32[]{:S(2)}, u32[]{:S(2)}) collective-permute-start(bf16[2,37632]{1,0:T(2,128)(2,1)S(1)} %broadcast_select_fusion.2), channel_id=1, source_target_pairs={{0,16},{1,17},{2,18},{3,19},{4,20},{5,21},{6,22},{7,23},{8,24},{9,... | collective-permute-start | bytes 451592 | tf_op jit(solution)/shard_map/ppermute | solution.py:410
  300.5 16.5 %collective-permute-start.32 = (bf16[8,2,48,768]{3,2,0,1:T(8,128)(2,1)}, bf16[8,2,48,768]{3,2,0,1:T(8,128)(2,1)}, u32[]{:S(2)}, u32[]{:S(2)}) collective-permute-start(bf16[8,2,48,768]{3,2,0,1:T(8,128)(2,1)} %fusion.4), channel_id=1, source_target_pairs={{0,4},{1,3},{2,6},{3,1},{4,0},{5,7},{6,2},{7,5},{8,12},{9,11},{10,... | collective-permute-start | bytes 3538952 | tf_op jit(solution)/shard_map/ppermute | solution.py:414
  307.5 28.5 %collective-permute-start.25 = (bf16[8,2,48,768]{3,2,0,1:T(8,128)(2,1)}, bf16[8,2,48,768]{3,2,0,1:T(8,128)(2,1)}, u32[]{:S(2)}, u32[]{:S(2)}) collective-permute-start(bf16[8,2,48,768]{3,2,0,1:T(8,128)(2,1)} %fusion.5), channel_id=1, source_target_pairs={{0,4},{1,3},{2,6},{3,1},{4,0},{5,7},{6,2},{7,5},{8,12},{9,11},{10,... | collective-permute-start | bytes 3538952 | tf_op jit(solution)/shard_map/ppermute | solution.py:414
  317.1 19.0 %copy-start.2 = (f32[16,1,48,768]{3,2,0,1:T(8,128)S(1)}, f32[16,1,48,768]{3,2,0,1:T(8,128)}, u32[]{:S(2)}) copy-start(f32[16,1,48,768]{3,2,0,1:T(8,128)} %copy-done.1) | copy-start | bytes 7077892
  317.1 19.0 %copy-start.4 = (f32[16,1,48,768]{3,2,0,1:T(8,128)S(1)}, f32[16,1,48,768]{3,2,0,1:T(8,128)}, u32[]{:S(2)}) copy-start(f32[16,1,48,768]{3,2,0,1:T(8,128)} %copy-done.3) | copy-start | bytes 7077892
  319.1 18.4 %copy-start.5 = (f32[8,2,48,768]{3,2,0,1:T(8,128)}, f32[8,2,48,768]{3,2,0,1:T(8,128)S(1)}, u32[]{:S(2)}) copy-start(f32[8,2,48,768]{3,2,0,1:T(8,128)S(1)} %fusion.1) | copy-start | bytes 7077892
  319.2 23.0 %collective-permute-start.33 = (bf16[4,2,48,768]{3,2,0,1:T(8,128)(2,1)S(1)}, bf16[4,2,48,768]{3,2,0,1:T(8,128)(2,1)}, u32[]{:S(2)}, u32[]{:S(2)}) collective-permute-start(bf16[4,2,48,768]{3,2,0,1:T(8,128)(2,1)S(1)} %slice.367), channel_id=1, source_target_pairs={{0,2},{1,5},{2,0},{3,7},{4,6},{5,1},{6,4},{7,3},{8,10},{9,13},{10,... | collective-permute-start | bytes 1769480 | tf_op jit(solution)/shard_map/ppermute | solution.py:414
  338.4 10.2 %collective-permute-start.26 = (bf16[4,2,48,768]{3,2,0,1:T(8,128)(2,1)}, bf16[4,2,48,768]{3,2,0,1:T(8,128)(2,1)}, u32[]{:S(2)}, u32[]{:S(2)}) collective-permute-start(bf16[4,2,48,768]{3,2,0,1:T(8,128)(2,1)} %slice.368), channel_id=1, source_target_pairs={{0,2},{1,5},{2,0},{3,7},{4,6},{5,1},{6,4},{7,3},{8,10},{9,13},{10,... | collective-permute-start | bytes 1769480 | tf_op jit(solution)/shard_map/ppermute | solution.py:414
  344.5 20.7 %collective-permute-start.34 = (bf16[2,2,48,768]{3,2,0,1:T(8,128)(2,1)}, bf16[2,2,48,768]{3,2,0,1:T(8,128)(2,1)}, u32[]{:S(2)}, u32[]{:S(2)}) collective-permute-start(bf16[2,2,48,768]{3,2,0,1:T(8,128)(2,1)} %slice.369), channel_id=1, source_target_pairs={{0,16},{1,17},{2,18},{3,19},{4,20},{5,21},{6,22},{7,23},{8,24},{9,... | collective-permute-start | bytes 884744 | tf_op jit(solution)/shard_map/ppermute | solution.py:414
  350.9 18.3 %copy-start.10 = (f32[4,2,48,768]{3,2,0,1:T(8,128)S(1)}, f32[4,2,48,768]{3,2,0,1:T(8,128)}, u32[]{:S(2)}) copy-start(f32[4,2,48,768]{3,2,0,1:T(8,128)} %copy-done.9) | copy-start | bytes 3538948
  350.9 18.3 %collective-permute-start.27 = (bf16[2,2,48,768]{3,2,0,1:T(8,128)(2,1)S(1)}, bf16[2,2,48,768]{3,2,0,1:T(8,128)(2,1)}, u32[]{:S(2)}, u32[]{:S(2)}) collective-permute-start(bf16[2,2,48,768]{3,2,0,1:T(8,128)(2,1)S(1)} %slice.370), channel_id=1, source_target_pairs={{0,16},{1,17},{2,18},{3,19},{4,20},{5,21},{6,22},{7,23},{8,24},{9,... | collective-permute-start | bytes 884744 | tf_op jit(solution)/shard_map/ppermute | solution.py:414
  366.5 6.9 %collective-permute-start.35 = (bf16[1,2,48,768]{3,2,0,1:T(8,128)(2,1)S(1)}, bf16[1,2,48,768]{3,2,0,1:T(8,128)(2,1)S(1)}, u32[]{:S(2)}, u32[]{:S(2)}) collective-permute-start(bf16[1,2,48,768]{3,2,0,1:T(8,128)(2,1)S(1)} %slice.371), channel_id=1, source_target_pairs={{0,8},{1,9},{2,10},{3,11},{4,12},{5,13},{6,14},{7,15},{8,0},{9,1},... | collective-permute-start | bytes 442376 | tf_op jit(solution)/shard_map/ppermute | solution.py:414
  370.2 5.2 %collective-permute-start.28 = (bf16[1,2,48,768]{3,2,0,1:T(8,128)(2,1)S(1)}, bf16[1,2,48,768]{3,2,0,1:T(8,128)(2,1)S(1)}, u32[]{:S(2)}, u32[]{:S(2)}) collective-permute-start(bf16[1,2,48,768]{3,2,0,1:T(8,128)(2,1)S(1)} %slice.372), channel_id=1, source_target_pairs={{0,8},{1,9},{2,10},{3,11},{4,12},{5,13},{6,14},{7,15},{8,0},{9,1},... | collective-permute-start | bytes 442376 | tf_op jit(solution)/shard_map/ppermute | solution.py:414
  375.5 1.4 collective-permute-start.29
  378.5 13.0 %copy-start.43 = (f32[24]{0:T(128)}, f32[24]{0:T(128)S(1)}, u32[]{:S(2)}) copy-start(f32[24]{0:T(128)S(1)} %get-tuple-element.194) | copy-start | bytes 292
  381.7 1.2 collective-permute-start.41
  382.9 4.2 %collective-permute-start.42 = (f32[13060]{0:T(1024)S(1)}, f32[13060]{0:T(1024)S(1)}, u32[]{:S(2)}, u32[]{:S(2)}) collective-permute-start(f32[13060]{0:T(1024)S(1)} %add.229), channel_id=1, source_target_pairs={{0,2},{1,3},{2,0},{3,1},{4,6},{5,7},{6,4},{7,5},{8,10},{9,11},{10,... | collective-permute-start | bytes 156728 | tf_op jit(solution)/shard_map/ppermute | solution.py:410
  387.1 4.2 %collective-permute-start.43 = (f32[13060]{0:T(1024)S(1)}, f32[13060]{0:T(1024)S(1)}, u32[]{:S(2)}, u32[]{:S(2)}) collective-permute-start(f32[13060]{0:T(1024)S(1)} %add.230), channel_id=1, source_target_pairs={{0,4},{1,5},{2,6},{3,7},{4,0},{5,1},{6,2},{7,3},{8,12},{9,13},{10,... | collective-permute-start | bytes 156728 | tf_op jit(solution)/shard_map/ppermute | solution.py:410
  391.4 4.2 %collective-permute-start.44 = (f32[13060]{0:T(1024)S(1)}, f32[13060]{0:T(1024)S(1)}, u32[]{:S(2)}, u32[]{:S(2)}) collective-permute-start(f32[13060]{0:T(1024)S(1)} %add.231), channel_id=1, source_target_pairs={{0,8},{1,9},{2,10},{3,11},{4,12},{5,13},{6,14},{7,15},{8,0},{9,1},... | collective-permute-start | bytes 156728 | tf_op jit(solution)/shard_map/ppermute | solution.py:410
  395.6 7.8 %collective-permute-start.45 = (f32[13060]{0:T(1024)S(1)}, f32[13060]{0:T(1024)S(1)}, u32[]{:S(2)}, u32[]{:S(2)}) collective-permute-start(f32[13060]{0:T(1024)S(1)} %add.232), channel_id=1, source_target_pairs={{0,16},{1,17},{2,18},{3,19},{4,20},{5,21},{6,22},{7,23},{8,24},{9,... | collective-permute-start | bytes 156728 | tf_op jit(solution)/shard_map/ppermute | solution.py:410
  401.5 12.0 %copy-start.19 = (f32[73728]{0:T(1024)}, f32[73728]{0:T(1024)S(1)}, u32[]{:S(2)}) copy-start(f32[73728]{0:T(1024)S(1)} %reshape_reshape_squeeze.3) | copy-start | bytes 884740
  402.1 12.1 %copy-start.18 = (f32[73728]{0:T(1024)S(1)}, f32[73728]{0:T(1024)}, u32[]{:S(2)}) copy-start(f32[73728]{0:T(1024)} %param.16) | copy-start | bytes 884740
  403.2 13.1 %copy-start.25 = (f32[73728]{0:T(1024)}, f32[73728]{0:T(1024)S(1)}, u32[]{:S(2)}) copy-start(f32[73728]{0:T(1024)S(1)} %reshape_reshape.3) | copy-start | bytes 884740
  403.3 12.4 %copy-start.29 = (f32[2352]{0:T(1024)S(1)}, f32[2352]{0:T(1024)}, u32[]{:S(2)}) copy-start(f32[2352]{0:T(1024)} %param.14) | copy-start | bytes 28228
  403.3 12.4 %copy-start.31 = (f32[2352]{0:T(1024)S(1)}, f32[2352]{0:T(1024)}, u32[]{:S(2)}) copy-start(f32[2352]{0:T(1024)} %get-tuple-element.181) | copy-start | bytes 28228
  403.3 13.1 %copy-start.27 = (f32[2,768]{1,0:T(2,128)S(1)}, f32[2,768]{1,0:T(2,128)}, u32[]{:S(2)}) copy-start(f32[2,768]{1,0:T(2,128)} %gains.5) | copy-start | bytes 18436
  403.3 13.0 %copy-start.47 = (f32[2]{0:T(128)S(1)}, f32[2]{0:T(128)}, u32[]{:S(2)}) copy-start(f32[2]{0:T(128)} %add_sqrt_fusion) | copy-start | bytes 28
  405.5 12.1 %copy-start.32 = (f32[2,768]{1,0:T(2,128)}, f32[2,768]{1,0:T(2,128)S(1)}, u32[]{:S(2)}) copy-start(f32[2,768]{1,0:T(2,128)S(1)} %get-tuple-element.183) | copy-start | bytes 18436
  405.5 12.1 %copy-start.33 = (f32[2,768]{1,0:T(2,128)}, f32[2,768]{1,0:T(2,128)S(1)}, u32[]{:S(2)}) copy-start(f32[2,768]{1,0:T(2,128)S(1)} %get-tuple-element.184) | copy-start | bytes 18436
  (33 other events, 167.4 us)
